TPU v7x, 32 devices: a whole 2x2x4 slice. The times are simulated.
32 devices in a mesh: parts: 2 (over x), tm: 16 (over z, y, core).
Axes of the slice: x: 2, y: 2, z: 4, core: 2. Of those that a mesh axis runs over, the one named last changes fastest.
Arguments:
- observations: float32 [256, 2048], P(('parts', 'tm')), parts along dimension 0, may hold values from -6 to 6
- outage_mask: int32 [256, 16], P(('parts', 'tm')), parts along dimension 0, may hold values 0 or 1
- group_length: int32 [32], P(('parts', 'tm')), parts along dimension 0, may hold values from 1 to 8, 96 in all
- prior_mean: float32 [4096], P('parts'), parts along dimension 0, may hold values from -8 to 8
- transition: float32 [16, 128, 128], replicated, may hold values from -1 to 1, as said below
- filter_gain: float32 [16, 128, 128], replicated, may hold values from -1 to 1, as said below
- smoother_gain: float32 [16, 128, 128], replicated, may hold values from -1 to 1, as said below
Outputs:
- smoothed: float32 [256, 2048], P(('parts', 'tm')), parts along dimension 0
There are 2 independent parts, one for each index of `parts`. A program takes and returns all parts, laid end to end along the dimension named above; an argument that names none is the same for every part. Nothing has to cross between parts.
Inputs may be any that keep to these rules, and one draw needn't show every extreme that they name: `group_length`: live steps of each tm index; they sum to 96 and one entry equals 8. `transition`: nonzero only between states 2p and 2p + 1 of a block; spectral norm below 1. `filter_gain`: Symmetric, eigenvalues between 0 and 1. `smoother_gain`: spectral norm below 1.
All inputs are finite; a program needn't handle non-finite values. No bound on the sum of `outage_mask` or of `group_length` on one device may be relied on, other than what follows from the above.
Results may differ from a plain program's by a relative error of at most 0.0003.
Values sent between devices are 32-bit elements; how exact they have to be, the bound alone decides.
A program may use at most 320 MiB of HBM per device.

v0:
```python
import jax
import jax.numpy as jnp
from jax import lax
from jax.sharding import PartitionSpec as P

highest = lax.Precision.HIGHEST


def carried_in(part, axis, combine, identity, reverse):
    count = lax.axis_size(axis)
    place = lax.axis_index(axis)
    ahead = count - 1 - place if reverse else place
    gathered = jax.tree.map(lambda a: lax.all_gather(a, axis), part)
    state = jax.tree.map(lambda a, e: jnp.zeros_like(a) + jnp.asarray(e, a.dtype), part, identity)

    def one(hop, state):
        source = count - 1 - hop if reverse else hop
        return combine(
            state, jax.tree.map(lambda a: lax.dynamic_index_in_dim(a, source, 0, False), gathered)
        )

    return lax.fori_loop(0, ahead, one, state)


def mat_mul(left, right):
    return jnp.einsum("bij,bjk->bik", left, right, precision=highest)


def mat_vec(matrix, vector):
    return jnp.einsum("bij,bj->bi", matrix, vector, precision=highest)


def compose(earlier, later_part):
    return (mat_mul(later_part[0], earlier[0]), mat_vec(later_part[0], earlier[1]) + later_part[1])


def shards(
    observations, outage_mask, group_length, prior_mean, transition, filter_gain, smoother_gain
):
    capacity = observations.shape[0]
    nblocks = transition.shape[0]
    width = transition.shape[1]
    identity_mat = jnp.eye(width, dtype=jnp.float32)
    identity_all = jnp.broadcast_to(identity_mat, transition.shape)
    updated = mat_mul(identity_mat - filter_gain, transition)
    back_keep = identity_mat - mat_mul(smoother_gain, transition)
    readings = observations.reshape(capacity, nblocks, width)
    length = group_length[0]
    slot_index = jnp.arange(capacity, dtype=jnp.int32)
    alive_slot = slot_index < length
    observed = (outage_mask == 1) & alive_slot[:, None]
    gain_terms = jnp.einsum("bij,tbj->tbi", filter_gain, readings, precision=highest)
    gain_terms = jnp.where(observed[:, :, None], gain_terms, jnp.float32(0.0))
    step_mats = jnp.where(observed[:, :, None, None], updated[None], transition[None])
    step_mats = jnp.where(alive_slot[:, None, None, None], step_mats, identity_mat[None, None])
    start_state = prior_mean.reshape(nblocks, width)
    zero_state = jnp.zeros((nblocks, width), jnp.float32)
    is_last = lax.axis_index("tm") == lax.axis_size("tm") - 1

    def compose_local(carried, inputs):
        step_mat, gain_term = inputs
        offset = mat_vec(step_mat, carried[1]) + gain_term
        return ((mat_mul(step_mat, carried[0]), offset), None)

    (group_map, group_offset), _ = lax.scan(
        compose_local, (identity_all, zero_state), (step_mats, gain_terms)
    )
    before_map, before_offset = carried_in(
        (group_map, group_offset), "tm", compose, (identity_all, zero_state), False
    )
    entry_state = mat_vec(before_map, start_state) + before_offset

    def forward(state, inputs):
        step_mat, gain_term, is_alive = inputs
        moved_state = mat_vec(step_mat, state) + gain_term
        moved_state = jnp.where(is_alive, moved_state, state)
        return (moved_state, moved_state)

    _, filtered = lax.scan(forward, entry_state, (step_mats, gain_terms, alive_slot))
    is_end = is_last & (slot_index == length - 1)

    def backward_run(later_start):

        def backward(later_state, inputs):
            state, is_alive, end_slot = inputs
            recurred = mat_vec(back_keep, state) + mat_vec(smoother_gain, later_state)
            result = jnp.where(end_slot, state, recurred)
            next_state = jnp.where(is_alive, result, later_state)
            return (next_state, jnp.where(is_alive, result, jnp.float32(0.0)))

        return lax.scan(backward, later_start, (filtered, alive_slot, is_end), reverse=True)

    group_back, _ = backward_run(zero_state)
    power_result = identity_all
    power_mat = smoother_gain
    bit_count = capacity.bit_length()
    for bit_index in range(bit_count):
        use_bit = length >> bit_index & 1 == 1
        power_result = jnp.where(use_bit, mat_mul(power_result, power_mat), power_result)
        if bit_index + 1 < bit_count:
            power_mat = mat_mul(power_mat, power_mat)
    back_map = jnp.where(is_last, jnp.float32(0.0), power_result)
    after_map, after_offset = carried_in(
        (back_map, group_back), "tm", compose, (identity_all, zero_state), True
    )
    _, smoothed = backward_run(after_offset)
    return smoothed.reshape(capacity, nblocks * width)


def solution(mesh):
    placed = (
        P(("parts", "tm"), None),
        P(("parts", "tm"), None),
        P(("parts", "tm")),
        P("parts"),
        P(),
        P(),
        P(),
    )
    return jax.shard_map(
        shards, mesh=mesh, in_specs=placed, out_specs=P(("parts", "tm"), None), check_vma=False
    )
```

profile of v0, /device:TPU:0, one launch (start us, length us, event | category | flops | bytes accessed | tf_op | source)
XLA Modules:
  0.0 486.1 jit_solution(12113377193240036252)
XLA Ops:
  8.1 2.9 fusion.27
  11.1 2.7 fusion.28
  13.8 5.2 %select_select_fusion = f32[8,16,128,128]{3,2,1,0:T(8,128)} fusion(f32[128,128]{1,0:T(8,128)S(1)} %fusion.33, f32[16,128,128]{2,1,0:T(8,128)} %param.23, f32[16,128,128]{2,1,0:T(8,128)S(1)} %fusion.28, pred[8]{0:T(512)(128)(4,1)S(1)} %iota_compare_fusion.1, pred[8,16]{1,0:T(8,128)(4,1)S(1)} %compare_and_fusion), kind=kLoop, calls=%fused_computation.39 | loop fusion | flops 4194304 | bytes 10551432 | tf_op jit(solution)/shard_map/jit(_where)/select_n | solution.py:55
  19.1 44.0 %while.86 = (s32[]{:T(128)}, f32[16,128,128]{2,1,0:T(8,128)S(1)}, f32[16,128]{1,0:T(8,128)S(1)}, f32[8,16,128,128]{3,2,1,0:T(8,128)}, f32[8,16,128]{2,1,0:T(8,128)S(1)}, /*index=5*/s32[]{:T(128)}, s32[]{:T(128)}) while((s32[]{:T(128)}, f32[16,128,128]{2,1,0:T(8,128)S(1)}, f32[16,128]{1,0:T(8,128)S(1)}, ...), condition=%wide.region_1.2_spmd.clone, body=%wide.region_0.1_spmd.clone.sunk | while | flops 405803008 | bytes 6349915 | solution.py:65
  19.2 3.0 fusion.130
  22.3 2.4 fusion.129
  24.7 3.0 fusion.130
  27.8 2.4 fusion.129
  30.2 3.0 fusion.130
  33.3 2.4 fusion.129
  35.7 3.0 fusion.130
  38.8 2.4 fusion.129
  41.2 3.0 fusion.130
  44.3 2.4 fusion.129
  46.7 3.0 fusion.130
  49.8 2.4 fusion.129
  52.2 3.0 fusion.130
  55.3 2.4 fusion.129
  57.7 3.0 fusion.130
  60.8 2.4 fusion.129
  71.4 2.2 fusion.26
  73.6 24.4 %all-gather.2 = f32[256,128]{1,0:T(8,128)S(1)} all-gather(f32[16,128]{1,0:T(8,128)S(1)} %get-tuple-element.485), channel_id=4, replica_groups=mesh['parts'=2,'tm'=16] {'tm'}, dimensions={0}, use_global_device_ids=true | all-gather | bytes 139264 | tf_op jit(solution)/shard_map/all_gather | solution.py:13
  99.2 95.8 %all-gather.9.cloned.1.call-done = f32[256,128,128]{2,1,0:T(8,128)} async-done(((f32[16,128,128]{2,1,0:T(8,128)}), f32[256,128,128]{2,1,0:T(8,128)}) %all-gather.9.cloned.1.call-update) | async-done | bytes 16777232 | tf_op jit(solution)/shard_map/all_gather | solution.py:13
  197.5 34.1 %while.83 = (s32[]{:T(128)}, f32[16,128]{1,0:T(8,128)S(1)}, f32[8,16,128]{2,1,0:T(8,128)S(1)}, pred[8]{0:T(512)(128)(4,1)S(1)}, f32[8,16,128,128]{3,2,1,0:T(8,128)}, /*index=5*/f32[8,16,128]{2,1,0:T(8,128)S(1)}, s32[]{:T(128)}) while((s32[]{:T(128)}, f32[16,128]{1,0:T(8,128)S(1)}, f32[8,16,128]{2,1,0:T(8,128)S(1)}, pred[8]{0:T(512)(128)(4,1)S(1)}, ...), condition=%wide.region_5.6_spmd, body=%wide.region_4.5_spmd.sunk | while | flops 3149826 | bytes 1106520 | solution.py:79
  197.6 2.9 fusion.115
  201.8 3.1 fusion.115
  206.2 2.9 fusion.115
  210.4 3.0 fusion.115
  214.6 3.0 fusion.115
  218.9 2.9 fusion.115
  223.1 3.0 fusion.115
  227.4 2.9 fusion.115
  231.6 49.6 %while.87 = (s32[]{:T(128)}, f32[16,128]{1,0:T(8,128)S(1)}, pred[8]{0:T(512)(128)(4,1)S(1)}, pred[8]{0:T(512)(128)(4,1)S(1)}, f32[8,16,128]{2,1,0:T(8,128)S(1)},...) while((s32[]{:T(128)}, f32[16,128]{1,0:T(8,128)S(1)}, ...), condition=%wide.region_7.8_spmd.clone, body=%wide.region_6.7_spmd.clone.sunk | while | flops 6301700 | bytes 2203794 | solution.py:91
  231.7 1.7 fusion.135
  244.1 1.7 fusion.135
  250.3 1.7 fusion.135
  262.7 1.7 fusion.135
  275.1 1.7 fusion.135
  281.2 97.4 %all-gather.3 = f32[256,128]{1,0:T(8,128)S(1)} all-gather(f32[16,128]{1,0:T(8,128)S(1)} %get-tuple-element.489), channel_id=5, replica_groups=mesh['parts'=2,'tm'=16] {'tm'}, dimensions={0}, use_global_device_ids=true | all-gather | bytes 139264 | tf_op jit(solution)/shard_map/all_gather | solution.py:13
  378.6 44.5 %while.84 = (s32[]{:T(128)}, f32[16,128]{1,0:T(8,128)S(1)}, s32[]{:T(128)}, f32[16,16,128,128]{3,2,1,0:T(8,128)}, f32[16,16,128]{2,1,0:T(8,128)S(1)}, /*index=5*/s32[]{:T(128)}, s32[]{:T(128)}, s32[]{:T(128)}, s32[]{:T(128)}) while((s32[]{:T(128)}, f32[16,128]{1,0:T(8,128)S(1)}, s32[]{:T(128)}, f32[16,16,128,128]{3,2,1,0:T(8,128)}, ...), condition=%wide.region_9.10_spmd, body=%wide.region_8.9_spmd.sunk | while | flops 3147782 | bytes 1089683 | solution.py:22
  378.6 2.9 fusion.118
  381.6 3.0 fusion.118
  384.6 3.0 fusion.118
  387.5 3.0 fusion.118
  390.5 3.0 fusion.118
  393.5 3.0 fusion.118
  396.4 3.0 fusion.118
  399.4 3.0 fusion.118
  402.4 3.0 fusion.118
  405.3 3.0 fusion.118
  408.3 3.0 fusion.118
  411.3 3.0 fusion.118
  414.2 3.0 fusion.118
  417.2 3.0 fusion.118
  420.2 3.0 fusion.118
  423.2 55.5 %while.85 = (s32[]{:T(128)}, f32[16,128]{1,0:T(8,128)S(1)}, f32[8,16,128]{2,1,0:T(8,128)S(1)}, pred[8]{0:T(512)(128)(4,1)S(1)}, pred[8]{0:T(512)(128)(4,1)S(1)},...) while((s32[]{:T(128)}, f32[16,128]{1,0:T(8,128)S(1)}, ...), condition=%wide.region_11.12_spmd, body=%wide.region_10.11_spmd.sunk | while | flops 6299651 | bytes 2211976 | solution.py:91
  423.2 1.7 fusion.123
  430.1 1.7 fusion.123
  437.1 1.7 fusion.123
  444.0 1.7 fusion.123
  450.9 1.7 fusion.123
  457.9 1.7 fusion.123
  464.8 1.7 fusion.123
  471.7 1.7 fusion.123
  (194 shorter events, 106.6 us)
Async XLA Ops:
  6.5 1.6 copy-start
  6.5 188.4 %all-gather.9.cloned.1.call-start = ((), (), s32[]{:S(2)}) async-start(), calls=%async_computation.1 | async-start | bytes 17825792 | tf_op jit(solution)/shard_map/all_gather | solution.py:13
  19.1 45.4 %copy-start.1 = (f32[16,128,128]{2,1,0:T(8,128)S(1)}, f32[16,128,128]{2,1,0:T(8,128)}, u32[]{:S(2)}) copy-start(f32[16,128,128]{2,1,0:T(8,128)} %param.25) | copy-start | bytes 3145732
  63.2 1.1 copy-start.2
  64.2 314.4 %all-gather.7.cloned.1.call-start = ((), (), s32[]{:S(2)}) async-start(), calls=%async_computation | async-start | bytes 17825792 | tf_op jit(solution)/shard_map/all_gather | solution.py:13
  66.7 31.4 %copy-start.3 = (f32[16,128,128]{2,1,0:T(8,128)S(1)}, f32[16,128,128]{2,1,0:T(8,128)}, u32[]{:S(2)}) copy-start(f32[16,128,128]{2,1,0:T(8,128)} %param.23) | copy-start | bytes 3145732
  195.1 0.7 copy-start.4
Sparse Core Ops, SparseCore 0:
  64.3 130.5 all-gather.8
  197.1 125.0 all-gather.6
where the time goes:
time: 489 us; the launch traced here: 486 us
  matrix products  184 us (38%)
  blocking collectives  122 us (25%)
  waiting for transfers between devices  95.8 us (20%)
  other arithmetic  39.1 us (8%)
  local copies, waits for them, and re-layouts  29.8 us (6%)
  between operations  14.3 us (3%)
    dot_general x64, matrix products, mat_vec(): return jnp.einsum('bij,bj->bi', matrix, vector, precision=highest)  149 us
    all_gather x2, blocking collectives, carried_in(): gathered = jax.tree.map(lambda a: lax.all_gather(a, axis), part)  122 us
    all_gather x2, waiting for transfers between devices, carried_in(): gathered = jax.tree.map(lambda a: lax.all_gather(a, axis), part)  95.8 us
    dot_general x17, matrix products, mat_mul(): return jnp.einsum('bij,bjk->bik', left, right, precision=highest)  32 us
    dynamic_slice x40, local copies, waits for them, and re-layouts, shards(): lax.scan(forward, entry_state, (step_mats, gain_terms, alive_slot))  26.3 us
    select_n x16, other arithmetic, backward(): next_state = jnp.where(is_alive, result, later_state)  16.5 us
    dynamic_update_slice x16, other arithmetic, shards(): lax.scan(forward, entry_state, (step_mats, gain_terms, alive_slot))  16.3 us
  transfers between devices with their start and end apart: 2, of which 1 were waited for; matrix products, arithmetic and copies ran while one was open for 20% of the time, Pallas kernels for 0%

commit v1 on v0

v1 whole, which is shorter than its diff:
```python
import functools

import jax
import jax.numpy as jnp
from jax import lax
from jax.experimental import pallas as pl
from jax.experimental.pallas import tpu as pltpu
from jax.sharding import PartitionSpec as P

highest = lax.Precision.HIGHEST
MESH = pl.DeviceIdType.MESH
WORD = 4


def mm(left, right):
    return jnp.dot(left, right, precision=highest, preferred_element_type=jnp.float32)


def radices_of(chunks):
    found, span = [], 1
    for radix in (4, 6, 4, 4, 4, 4):
        if span >= chunks:
            break
        found.append(radix)
        span *= radix
    return found


def iota(shape, axis):
    return lax.broadcasted_iota(jnp.int32, shape, axis)


def kernel(
    n,
    length_ref,
    mask_ref,
    obs_hbm,
    prior_ref,
    trans_hbm,
    filt_hbm,
    smooth_hbm,
    out_hbm,
    obs_v,
    stage,
    got,
    trans_v,
    filt_v,
    smooth_v,
    words,
    words_t,
    index_v,
    index_s,
    offsets,
    entries,
    buf_a,
    buf_b,
    result,
    load_sem,
    send_sem,
    recv_sem,
    send_sem2,
    recv_sem2,
    index_sem,
):
    cap = obs_v.shape[0]
    width = trans_v.shape[0]
    nblocks = trans_hbm.shape[0]
    share = n // nblocks
    slots = n * cap
    live = slots * 3 // 4
    chunks = live // WORD
    padded = -(-live // width) * width

    me = lax.axis_index("tm")
    block = me // share

    obs_load = pltpu.make_async_copy(obs_hbm, obs_v, load_sem.at[0])
    obs_load.start()
    loads = []
    for place, (source, target) in enumerate(
        ((trans_hbm, trans_v), (filt_hbm, filt_v), (smooth_hbm, smooth_v))
    ):
        load = pltpu.make_async_copy(source.at[block], target, load_sem.at[place + 1])
        load.start()
        loads.append(load)

    barrier = pltpu.get_barrier_semaphore()
    for step in range(1, n):
        pl.semaphore_signal(
            barrier, inc=1, device_id={"tm": lax.rem(me + step, n)}, device_id_type=MESH
        )

    length = length_ref[0]
    alive_here = (iota((cap, width), 0) < length).astype(jnp.float32)
    left_half = iota((cap, width), 1) < width // 2
    mask_f = mask_ref[...].astype(jnp.float32)
    for b in range(nblocks):
        seen = jnp.broadcast_to(mask_f[:, b : b + 1], (cap, width))
        stage[b, cap : 2 * cap, :] = jnp.where(left_half, seen * alive_here, alive_here)
    obs_load.wait()
    for b in range(nblocks):
        stage[b, 0:cap, :] = obs_v[:, b * width : (b + 1) * width]

    pl.semaphore_wait(barrier, n - 1)
    own_in = pltpu.make_async_copy(stage.at[block], got.at[me], recv_sem)
    own_in.start()
    for step in range(1, n):
        there = lax.rem(me + step, n)
        pltpu.make_async_remote_copy(
            src_ref=stage.at[there // share],
            dst_ref=got.at[me],
            send_sem=send_sem,
            recv_sem=recv_sem,
            device_id={"tm": there},
            device_id_type=MESH,
        ).start()

    for load in loads:
        load.wait()
    trans = trans_v[...]
    gain = filt_v[...]
    update = trans - mm(gain, trans)
    trans_t = trans.T
    update_t = update.T
    gain_t = gain.T
    smooth_t = smooth_v[...].T
    back_t = (iota((width, width), 0) == iota((width, width), 1)).astype(jnp.float32) - mm(
        trans_t, smooth_t
    )
    step_t = jnp.concatenate([update_t, trans_t], axis=1)
    square = mm(jnp.concatenate([trans, update], axis=0), jnp.concatenate([trans, update], axis=1))
    square_t = mm(
        jnp.concatenate([trans_t, update_t], axis=0), jnp.concatenate([trans_t, update_t], axis=1)
    )

    def tile(whole, row, column):
        return whole[row * width : (row + 1) * width, column * width : (column + 1) * width]

    pairs = [tile(square, hi, lo) for hi in range(2) for lo in range(2)]
    pairs_t = [tile(square_t, lo, hi) for hi in range(2) for lo in range(2)]
    pairs_row = jnp.concatenate(pairs, axis=1)
    pairs_t_row = jnp.concatenate(pairs_t, axis=1)
    for q in range(4):
        row = mm(pairs[q], pairs_row)
        row_t = mm(pairs_t[q], pairs_t_row)
        for p in range(4):
            words[4 * q + p] = row[:, p * width : (p + 1) * width]
            words_t[4 * p + q] = row_t[:, p * width : (p + 1) * width]

    radices = radices_of(chunks)
    levels = []
    base = smooth_t
    for radix in [WORD] + radices:
        powers = [base]
        while len(powers) < radix:
            have = len(powers)
            take = min(have, radix - have)
            more = mm(powers[-1], jnp.concatenate(powers[:take], axis=1) if take > 1 else powers[0])
            powers += [more[:, i * width : (i + 1) * width] for i in range(take)]
        levels.append(jnp.concatenate(powers[: radix - 1], axis=0))
        base = powers[radix - 1]

    pltpu.make_async_copy(got, got, recv_sem).wait()
    arrived = got[...]
    readings = arrived[:, 0:cap, :].reshape(slots, width)
    bits = arrived[:, cap : 2 * cap, :].reshape(slots, width)
    turned = pltpu.roll(bits, width // 2, 1)
    left = iota((slots, width), 1) < width // 2
    seen_slot = jnp.where(left, bits, turned)
    alive_slot = jnp.where(left, turned, bits)
    earlier = (iota((slots, slots), 1) < iota((slots, slots), 0)).astype(jnp.bfloat16)
    place = jnp.dot(
        earlier, alive_slot.astype(jnp.bfloat16), preferred_element_type=jnp.float32
    )
    pieces = []
    for first in range(0, padded, width):
        lane = iota((slots, width), 1) + first
        within = sum((lane >= s * chunks).astype(jnp.int32) for s in range(1, WORD))
        step_of = WORD * (lane - within * chunks) + within
        step_of = jnp.where(lane < live, step_of, -1)
        chosen = (alive_slot > 0.5) & (place.astype(jnp.int32) == step_of)
        pieces.append(chosen.astype(jnp.float32))
    spread = jnp.concatenate(pieces, axis=1) if len(pieces) > 1 else pieces[0]
    compact = mm(spread.T, jnp.concatenate([readings, seen_slot], axis=1))[:live]
    seen = [compact[s * chunks : (s + 1) * chunks, width:] > 0.5 for s in range(WORD)]
    index = sum(jnp.where(seen[s], 1 << s, 0) for s in range(WORD))
    index_v[...] = index
    index_copy = pltpu.make_async_copy(index_v, index_s, index_sem)
    index_copy.start()
    gained = mm(compact[:, :width], gain_t)
    gains = [
        jnp.where(seen[s], gained[s * chunks : (s + 1) * chunks], 0.0) for s in range(WORD)
    ]

    def advance(state, s):
        both = mm(state, step_t)
        return jnp.where(seen[s], both[:, :width], both[:, width:]) + gains[s]

    offset = gains[0]
    for s in range(1, WORD):
        offset = advance(offset, s)
    offsets[...] = offset
    index_copy.wait()

    eye = iota((width, width), 0) == iota((width, width), 1)
    group = 2
    entries[0:1, :] = prior_ref[:, pl.ds(pl.multiple_of(block * width, width), width)]

    def run(turn, state):
        for inner in range(group):
            c = turn * (2 * group) + 2 * inner
            terms = words[index_s[c, 0]] * state
            terms = terms + jnp.where(eye, offsets[pl.ds(c, 1), :], 0.0)
            column = jnp.sum(terms, axis=1, keepdims=True)
            entries[pl.ds(c + 1, 1), :] = jnp.sum(
                jnp.where(eye, column, 0.0), axis=0, keepdims=True
            )
            terms = words_t[index_s[c + 1, 0]] * column
            state = jnp.sum(terms, axis=0, keepdims=True) + offsets[pl.ds(c + 1, 1), :]
            entries[pl.ds(c + 2, 1), :] = state
        return state

    lax.fori_loop(0, chunks // (2 * group), run, entries[0:1, :])

    state = entries[0:chunks, :]
    filtered = []
    for s in range(WORD - 1):
        state = advance(state, s)
        filtered.append(state)
    filtered.append(entries[1 : chunks + 1, :])

    rows = jnp.concatenate(filtered, axis=0)
    recurred = mm(rows, back_t)
    is_end = iota((live, width), 0) == live - 1
    total = jnp.where(is_end, rows, recurred)

    tail = buf_a.shape[1] - chunks
    for s in range(WORD):
        buf_a[s, chunks:, :] = jnp.zeros((tail, width), jnp.float32)
        buf_b[s, chunks:, :] = jnp.zeros((tail, width), jnp.float32)
    stride = 1
    for level, radix in enumerate([WORD] + radices):
        buf = buf_a if level % 2 == 0 else buf_b
        for s in range(WORD):
            buf[s, 0:chunks, :] = total[s * chunks : (s + 1) * chunks]
        columns = []
        for i in range(1, radix):
            parts = []
            for s in range(WORD):
                ahead = s + i if level == 0 else s + i * stride
                parts.append(buf[ahead % WORD, pl.ds(ahead // WORD, chunks), :])
            columns.append(jnp.concatenate(parts, axis=0))
        total = total + mm(jnp.concatenate(columns, axis=1), levels[level])
        stride *= radix

    result[...] = mm(spread[:, :live], total).reshape(n, cap, width)

    column_of = pl.ds(pl.multiple_of(block * width, width), width)
    own_out = pltpu.make_async_copy(result.at[me], out_hbm.at[:, column_of], recv_sem2)
    own_out.start()
    for step in range(1, nblocks):
        there = lax.rem(me + step * share, n)
        pltpu.make_async_remote_copy(
            src_ref=result.at[there],
            dst_ref=out_hbm.at[:, column_of],
            send_sem=send_sem2,
            recv_sem=recv_sem2,
            device_id={"tm": there},
            device_id_type=MESH,
        ).start()
    sent = got.at[pl.ds(0, n - 1)]
    pltpu.make_async_copy(sent, sent, send_sem).wait()
    sent = result.at[pl.ds(0, nblocks - 1)]
    pltpu.make_async_copy(sent, sent, send_sem2).wait()
    pltpu.make_async_copy(out_hbm, out_hbm, recv_sem2).wait()


def shards(
    observations, outage_mask, group_length, prior_mean, transition, filter_gain, smoother_gain
):
    cap = observations.shape[0]
    nblocks, width, _ = transition.shape
    n = lax.axis_size("tm")
    chunks = n * cap * 3 // 4 // WORD
    reach = max([1] + [(r - 1) * s for r, s in zip(radices_of(chunks), strides_of(chunks))])
    tall = chunks + -(-reach // 8) * 8
    vmem, anywhere, smem = (
        pl.BlockSpec(memory_space=pltpu.VMEM),
        pl.BlockSpec(memory_space=pl.ANY),
        pl.BlockSpec(memory_space=pltpu.SMEM),
    )
    f32 = jnp.float32
    return pl.pallas_call(
        functools.partial(kernel, n),
        out_shape=jax.ShapeDtypeStruct(observations.shape, f32),
        in_specs=[smem, vmem, anywhere, vmem, anywhere, anywhere, anywhere],
        out_specs=anywhere,
        scratch_shapes=[
            pltpu.VMEM((cap, nblocks * width), f32),
            pltpu.VMEM((nblocks, 2 * cap, width), f32),
            pltpu.VMEM((n, 2 * cap, width), f32),
            pltpu.VMEM((width, width), f32),
            pltpu.VMEM((width, width), f32),
            pltpu.VMEM((width, width), f32),
            pltpu.VMEM((1 << WORD, width, width), f32),
            pltpu.VMEM((1 << WORD, width, width), f32),
            pltpu.VMEM((chunks, width), jnp.int32),
            pltpu.SMEM((chunks, width), jnp.int32),
            pltpu.VMEM((chunks, width), f32),
            pltpu.VMEM((chunks + 8, width), f32),
            pltpu.VMEM((WORD, tall, width), f32),
            pltpu.VMEM((WORD, tall, width), f32),
            pltpu.VMEM((n, cap, width), f32),
            pltpu.SemaphoreType.DMA((4,)),
            pltpu.SemaphoreType.DMA,
            pltpu.SemaphoreType.DMA,
            pltpu.SemaphoreType.DMA,
            pltpu.SemaphoreType.DMA,
            pltpu.SemaphoreType.DMA,
        ],
        compiler_params=pltpu.CompilerParams(
            collective_id=0, has_side_effects=True, vmem_limit_bytes=40 << 20
        ),
    )(
        group_length,
        outage_mask,
        observations,
        prior_mean.reshape(1, -1),
        transition,
        filter_gain,
        smoother_gain,
    )


def strides_of(chunks):
    strides, span = [], 1
    for radix in radices_of(chunks):
        strides.append(span)
        span *= radix
    return strides


def solution(mesh):
    placed = (
        P(("parts", "tm"), None),
        P(("parts", "tm"), None),
        P(("parts", "tm")),
        P("parts"),
        P(),
        P(),
        P(),
    )
    return jax.shard_map(
        shards, mesh=mesh, in_specs=placed, out_specs=P(("parts", "tm"), None), check_vma=False
    )
```

time: 489 us -> 28 us (0.06)
  matrix products: 184 us -> 0 us
  blocking collectives: 122 us -> 0 us
  waiting for transfers between devices: 95.8 us -> 0 us
  other arithmetic: 39.1 us -> 0 us
  local copies, waits for them, and re-layouts: 29.8 us -> 6.52 us
  Pallas kernels: 0 us -> 20.4 us
  between operations: 14.3 us -> 0.67 us
    dot_general x82 -> x0, matrix products: 184 us -> none  [the longest x64 149 us: mat_vec(): return jnp.einsum('bij,bj->bi', matrix, vector, precision=highest)]
    all_gather x2 -> x0, blocking collectives: 122 us -> none  [carried_in(): gathered = jax.tree.map(lambda a: lax.all_gather(a, axis), part)]
    all_gather x2 -> x0, waiting for transfers between devices: 95.8 us -> none  [carried_in(): gathered = jax.tree.map(lambda a: lax.all_gather(a, axis), part)]
    dynamic_slice x56 -> x0, local copies, waits for them, and re-layouts: 26.4 us -> none  [the longest x40 26.3 us: shards(): lax.scan(forward, entry_state, (step_mats, gain_terms, alive_slot))]
    select_n x17 -> x0, other arithmetic: 21.8 us -> none  [the longest x16 16.5 us: backward(): next_state = jnp.where(is_alive, result, later_state)]
    pallas_call x0 -> x1, Pallas kernels: none -> 20.4 us  [shards(): pl.pallas_call(functools.partial(kernel, n), out_shape=jax.ShapeDtypeStru...]
    dynamic_update_slice x16 -> x0, other arithmetic: 16.3 us -> none  [shards(): lax.scan(forward, entry_state, (step_mats, gain_terms, alive_slot))]
  transfers between devices with their start and end apart: 2 -> 0, of which waited for: 1 -> 0; matrix products, arithmetic and copies ran while one was open for 20% -> 0% of each run, Pallas kernels for 0% -> 0%
where the time goes in v1:
time: 28 us; the launch traced here: 27.6 us
  Pallas kernels  20.4 us (73%)
  local copies, waits for them, and re-layouts  6.52 us (23%)
  between operations  0.67 us (2%)
    pallas_call x1, Pallas kernels, shards(): pl.pallas_call(functools.partial(kernel, n), out_shape=jax.ShapeDtypeStru...  20.4 us
    unnamed x13, local copies, waits for them, and re-layouts  6.52 us

profile of v1, /device:TPU:0, one launch (start us, length us, event | category | flops | bytes accessed | tf_op | source)
XLA Modules:
  0.0 27.6 jit_solution(6758690325561374558)
XLA Ops:
  0.7 0.0 copy-start
  0.7 1.2 %copy-done = f32[16,128,128]{2,1,0:T(8,128)S(1)} copy-done((f32[16,128,128]{2,1,0:T(8,128)S(1)}, f32[16,128,128]{2,1,0:T(8,128)}, u32[]{:S(2)}) %copy-start) | copy-done | bytes 1048600
  1.9 0.0 copy-start.1
  1.9 1.2 %copy-done.1 = f32[16,128,128]{2,1,0:T(8,128)S(1)} copy-done((f32[16,128,128]{2,1,0:T(8,128)S(1)}, f32[16,128,128]{2,1,0:T(8,128)}, u32[]{:S(2)}) %copy-start.1) | copy-done | bytes 1048600
  3.1 0.0 copy-start.2
  3.1 1.2 %copy-done.2 = f32[16,128,128]{2,1,0:T(8,128)S(1)} copy-done((f32[16,128,128]{2,1,0:T(8,128)S(1)}, f32[16,128,128]{2,1,0:T(8,128)}, u32[]{:S(2)}) %copy-start.2) | copy-done | bytes 1048600
  4.3 0.0 copy-start.3
  4.3 0.8 %copy-done.3 = f32[8,2048]{1,0:T(8,128)S(1)} copy-done((f32[8,2048]{1,0:T(8,128)S(1)}, f32[8,2048]{1,0:T(8,128)}, u32[]{:S(2)}) %copy-start.3) | copy-done | bytes 65560
  5.2 0.0 copy-start.4
  5.2 0.7 %copy-done.4 = f32[2048]{0:T(1024)S(1)} copy-done((f32[2048]{0:T(1024)S(1)}, f32[2048]{0:T(1024)}, u32[]{:S(2)}) %copy-start.4) | copy-done | bytes 8216
  5.9 0.0 copy-start.5
  5.9 0.7 %copy-done.5 = s32[8,16]{1,0:T(8,128)S(1)} copy-done((s32[8,16]{1,0:T(8,128)S(1)}, s32[8,16]{1,0:T(8,128)}, u32[]{:S(2)}) %copy-start.5) | copy-done | bytes 536
  6.6 20.4 %shard_map.73 = f32[8,2048]{1,0:T(8,128)S(1)} custom-call(s32[1]{0:T(128)S(6)} %copy.9.length_ref, s32[8,16]{1,0:T(8,128)S(1)} %copy-done.5, f32[8,2048]{1,0:T(8,128)S(1)} %copy-done.3, f32[1,2048]{1,0:T(1,128)S(1)} %bitcast.1, f32[16,128,128]{2,1,0:T(8,128)S(1)} %copy-done, f32[16,128,128]{2,1,0:T(8,128)S(1)} %copy-done.1, f32[16,128,128]{2,1,0:T(8,128)S(1)} %copy-done.2), custom_call_target="tpu_custom_call" | custom-call | tf_op jit(solution)/shard_map/pallas_call | solution.py:293
  27.0 0.6 %copy.10 = f32[8,2048]{1,0:T(8,128)} copy(f32[8,2048]{1,0:T(8,128)S(1)} %shard_map.73) | data formatting | bytes 131072
Async XLA Ops:
  0.7 1.2 %copy-start = (f32[16,128,128]{2,1,0:T(8,128)S(1)}, f32[16,128,128]{2,1,0:T(8,128)}, u32[]{:S(2)}) copy-start(f32[16,128,128]{2,1,0:T(8,128)} %trans_hbm.1) | copy-start | bytes 3145732
  1.9 1.2 %copy-start.1 = (f32[16,128,128]{2,1,0:T(8,128)S(1)}, f32[16,128,128]{2,1,0:T(8,128)}, u32[]{:S(2)}) copy-start(f32[16,128,128]{2,1,0:T(8,128)} %filt_hbm.1) | copy-start | bytes 3145732
  3.1 1.2 %copy-start.2 = (f32[16,128,128]{2,1,0:T(8,128)S(1)}, f32[16,128,128]{2,1,0:T(8,128)}, u32[]{:S(2)}) copy-start(f32[16,128,128]{2,1,0:T(8,128)} %smooth_hbm.1) | copy-start | bytes 3145732
  4.3 0.8 %copy-start.3 = (f32[8,2048]{1,0:T(8,128)S(1)}, f32[8,2048]{1,0:T(8,128)}, u32[]{:S(2)}) copy-start(f32[8,2048]{1,0:T(8,128)} %obs_hbm.1) | copy-start | bytes 196612
  5.2 0.7 %copy-start.4 = (f32[2048]{0:T(1024)S(1)}, f32[2048]{0:T(1024)}, u32[]{:S(2)}) copy-start(f32[2048]{0:T(1024)} %param.10) | copy-start | bytes 24580
  5.9 0.7 %copy-start.5 = (s32[8,16]{1,0:T(8,128)S(1)}, s32[8,16]{1,0:T(8,128)}, u32[]{:S(2)}) copy-start(s32[8,16]{1,0:T(8,128)} %mask_ref.1) | copy-start | bytes 1540

commit v2 on v1

v2 whole, which is shorter than its diff:
```python
import functools

import jax
import jax.numpy as jnp
from jax import lax
from jax.experimental import pallas as pl
from jax.experimental.pallas import tpu as pltpu
from jax.sharding import PartitionSpec as P

highest = lax.Precision.HIGHEST
MESH = pl.DeviceIdType.MESH
WORD = 3


def ready(weight):
    return weight


def mm(left, right):
    return jnp.dot(left, right, precision=highest, preferred_element_type=jnp.float32)


def choose(chosen, values):
    return jnp.dot(chosen, values, precision=highest, preferred_element_type=jnp.float32)


def radices_of(chunks):
    found, span = [], 1
    for radix in (6, 6, 4, 4, 4, 4):
        if span >= chunks:
            break
        found.append(radix)
        span *= radix
    return found


def iota(shape, axis):
    return lax.broadcasted_iota(jnp.int32, shape, axis)


def kernel(
    n,
    length_hbm,
    mask_hbm,
    obs_hbm,
    prior_hbm,
    trans_hbm,
    filt_hbm,
    smooth_hbm,
    out_hbm,
    length_s,
    mask_v,
    prior_v,
    obs_v,
    stage,
    got,
    trans_v,
    filt_v,
    smooth_v,
    words,
    words_t,
    index_v,
    index_s,
    offsets,
    entries,
    buf_a,
    buf_b,
    result,
    load_sem,
    send_sem,
    recv_sem,
    send_sem2,
    recv_sem2,
    index_sem,
):
    cap = obs_v.shape[0]
    width = trans_v.shape[0]
    half = width // 2
    nblocks = trans_hbm.shape[0]
    share = n // nblocks
    slots = n * cap
    live = slots * 3 // 4
    chunks = live // WORD
    padded = -(-live // width) * width

    me = lax.axis_index("tm")
    block = me // share

    loads = []
    for place, (source, target) in enumerate(
        (
            (length_hbm, length_s),
            (mask_hbm, mask_v),
            (obs_hbm, obs_v),
            (trans_hbm.at[block], trans_v),
            (filt_hbm.at[block], filt_v),
            (smooth_hbm.at[block], smooth_v),
            (prior_hbm, prior_v),
        )
    ):
        load = pltpu.make_async_copy(source, target, load_sem.at[place])
        load.start()
        loads.append(load)

    barrier = pltpu.get_barrier_semaphore()
    for step in range(1, n):
        pl.semaphore_signal(
            barrier, inc=1, device_id={"tm": lax.rem(me + step, n)}, device_id_type=MESH
        )

    loads[0].wait()
    loads[1].wait()
    length = length_s[0]
    alive_here = (iota((cap, width), 0) < length).astype(jnp.float32)
    lane = iota((cap, width), 1)
    left_half = lane < half
    own_slot = iota((cap, width), 0) * half + (lane - half) - me * cap
    alive_lanes = ((own_slot >= 0) & (own_slot < length)).astype(jnp.float32)
    mask_f = mask_v[...].astype(jnp.float32)
    for b in range(nblocks):
        seen = jnp.broadcast_to(mask_f[:, b : b + 1], (cap, width))
        stage[b, cap : 2 * cap, :] = jnp.where(left_half, seen * alive_here, alive_lanes)
    loads[2].wait()
    for b in range(nblocks):
        stage[b, 0:cap, :] = obs_v[:, b * width : (b + 1) * width]

    pl.semaphore_wait(barrier, n - 1)
    for step in range(1, n):
        there = lax.rem(me + step, n)
        pltpu.make_async_remote_copy(
            src_ref=stage.at[there // share],
            dst_ref=got.at[me],
            send_sem=send_sem,
            recv_sem=recv_sem,
            device_id={"tm": there},
            device_id_type=MESH,
        ).start()
    own_in = pltpu.make_async_copy(stage.at[block], got.at[me], recv_sem)
    own_in.start()

    for load in loads[3:]:
        load.wait()
    trans = trans_v[...]
    gain = filt_v[...]
    update = trans - mm(gain, ready(trans))
    trans_t = trans.T
    update_t = update.T
    gain_t = ready(gain.T)
    step_t = ready(jnp.concatenate([update_t, trans_t], axis=1))
    square = mm(
        jnp.concatenate([trans, update], axis=0),
        ready(jnp.concatenate([trans, update], axis=1)),
    )
    square_t = mm(
        jnp.concatenate([trans_t, update_t], axis=0),
        ready(jnp.concatenate([trans_t, update_t], axis=1)),
    )

    def tile(whole, row, column):
        return whole[row * width : (row + 1) * width, column * width : (column + 1) * width]

    pairs = [tile(square, hi, lo) for hi in range(2) for lo in range(2)]
    pairs_t = [tile(square_t, lo, hi) for hi in range(2) for lo in range(2)]
    cube = mm(
        jnp.concatenate([trans, update], axis=0), ready(jnp.concatenate(pairs, axis=1))
    )
    cube_t = mm(
        jnp.concatenate(pairs_t, axis=0),
        ready(jnp.concatenate([trans_t, update_t], axis=1)),
    )
    for last in range(2):
        for p in range(4):
            words[4 * last + p] = tile(cube, last, p)
            words_t[4 * last + p] = tile(cube_t, p, last)

    pltpu.make_async_copy(got, got, recv_sem).wait()
    arrived = got[...]
    readings = arrived[:, 0:cap, :].reshape(slots, width)
    bits = arrived[:, cap : 2 * cap, :].reshape(slots, width)
    seen_slot = jnp.where(iota((slots, width), 1) < half, bits, pltpu.roll(bits, half, 1))
    gained_slot = mm(readings, gain_t)
    alive_sum = jnp.sum(arrived[:, cap : 2 * cap, :], axis=0)
    alive_roll = pltpu.roll(alive_sum, half, 1)
    left_row = iota((1, width), 1) < half
    alive_row = jnp.concatenate(
        [
            jnp.where(left_row, alive_roll[2 * k : 2 * k + 1], alive_sum[2 * k + 1 : 2 * k + 2])
            for k in range(slots // width)
        ],
        axis=1,
    )
    earlier = (iota((slots, slots), 0) < iota((slots, slots), 1)).astype(jnp.bfloat16)
    place = jnp.dot(
        jnp.broadcast_to(alive_row, (16, slots)).astype(jnp.bfloat16),
        earlier,
        preferred_element_type=jnp.float32,
    )[0:1]
    place = jnp.where(alive_row > 0.5, place, -1.0)
    row = iota((padded, slots), 0)
    within = sum((row >= s * chunks).astype(jnp.int32) for s in range(1, WORD))
    step_of = WORD * (row - within * chunks) + within
    step_of = jnp.where(row < live, step_of, -2).astype(jnp.float32)
    gather = (jnp.broadcast_to(place, (padded, slots)) == step_of).astype(jnp.float32)
    compact = choose(gather, jnp.concatenate([gained_slot, seen_slot], axis=1))[:live]
    seen = [compact[s * chunks : (s + 1) * chunks, width:] > 0.5 for s in range(WORD)]
    index_v[...] = sum(jnp.where(seen[s], 1 << s, 0) for s in range(WORD))
    index_copy = pltpu.make_async_copy(index_v, index_s, index_sem)
    index_copy.start()
    gains = [
        jnp.where(seen[s], compact[s * chunks : (s + 1) * chunks, :width], 0.0)
        for s in range(WORD)
    ]

    def advance(state, s):
        both = mm(state, step_t)
        return jnp.where(seen[s], both[:, :width], both[:, width:]) + gains[s]

    offset = gains[0]
    for s in range(1, WORD):
        offset = advance(offset, s)
    offsets[...] = offset
    index_copy.wait()

    radices = [WORD] + radices_of(chunks)
    levels = []

    def powers_by_steps():
        base = smooth_v[...].T
        for level, radix in enumerate(radices):
            wanted = radix - 1 if level == len(radices) - 1 else radix
            powers = [base]
            while len(powers) < wanted:
                take = min(len(powers), wanted - len(powers))
                more = mm(powers[-1], ready(jnp.concatenate(powers[:take], axis=1)))
                powers += [more[:, i * width : (i + 1) * width] for i in range(take)]
                yield
            if level == 0:
                ends = mm(trans_t, ready(jnp.concatenate(powers, axis=1)))
                yield
                ends = [ends[:, i * width : (i + 1) * width] for i in range(radix)]
                eye_f = (iota((width, width), 0) == iota((width, width), 1)).astype(jnp.float32)
                starts = [l - e for l, e in zip([eye_f] + powers[: radix - 1], ends)]
                levels.append(ready(jnp.concatenate(starts, axis=0)))
                levels.append(ready(jnp.concatenate(ends, axis=1)))
            else:
                levels.append(ready(jnp.concatenate(powers[: radix - 1], axis=0)))
            base = powers[-1]

    side = powers_by_steps()

    eye = iota((width, width), 0) == iota((width, width), 1)
    state = prior_v[:, pl.ds(pl.multiple_of(block * width, width), width)]
    entries[0:1, :] = state
    for c in range(0, chunks, 2):
        terms = words[index_s[c, 0]] * state
        terms = terms + jnp.where(eye, offsets[c : c + 1, :], 0.0)
        column = jnp.sum(terms, axis=1, keepdims=True)
        entries[c + 1 : c + 2, :] = jnp.sum(jnp.where(eye, column, 0.0), axis=0, keepdims=True)
        terms = words_t[index_s[c + 1, 0]] * column
        state = jnp.sum(terms, axis=0, keepdims=True) + offsets[c + 1 : c + 2, :]
        entries[c + 2 : c + 3, :] = state
        next(side, None)
    for _ in side:
        pass

    state = entries[0:chunks, :]
    filtered = []
    for s in range(WORD - 1):
        state = advance(state, s)
        filtered.append(state)
    filtered.append(entries[1 : chunks + 1, :])
    newest = entries[chunks : chunks + 1, :]

    tail = buf_a.shape[1] - chunks
    for s in range(WORD):
        buf_a[s, chunks:, :] = jnp.zeros((tail, width), jnp.float32)
        buf_b[s, chunks:, :] = jnp.zeros((tail, width), jnp.float32)

    def ahead_of(buf, values, radix, stride):
        for s in range(WORD):
            buf[s, 0:chunks, :] = values[s]
        columns = []
        for i in range(1, radix):
            parts = []
            for s in range(WORD):
                later = s + i * stride
                parts.append(buf[later % WORD, later // WORD : later // WORD + chunks, :])
            columns.append(jnp.concatenate(parts, axis=0))
        return columns

    def by_step(rows):
        return [rows[s * chunks : (s + 1) * chunks] for s in range(WORD)]

    columns = [jnp.concatenate(filtered, axis=0)] + ahead_of(buf_a, filtered, WORD, 1)
    total = mm(jnp.concatenate(columns, axis=1), levels[0])
    finish = mm(jnp.broadcast_to(newest, (8, width)), levels[1])[0:1]
    is_end = iota((chunks, width), 0) == chunks - 1
    total = total + jnp.concatenate(
        [
            jnp.where(is_end, finish[:, i * width : (i + 1) * width], 0.0)
            for i in reversed(range(WORD))
        ],
        axis=0,
    )
    stride = WORD
    for level, radix in enumerate(radices[1:]):
        buf = buf_b if level % 2 == 0 else buf_a
        columns = ahead_of(buf, by_step(total), radix, stride)
        total = total + mm(jnp.concatenate(columns, axis=1), levels[level + 2])
        stride *= radix

    result[...] = choose(gather.T[:, :live], total).reshape(n, cap, width)

    column_of = pl.ds(pl.multiple_of(block * width, width), width)
    for step in range(1, nblocks):
        there = lax.rem(me + step * share, n)
        pltpu.make_async_remote_copy(
            src_ref=result.at[there],
            dst_ref=out_hbm.at[:, column_of],
            send_sem=send_sem2,
            recv_sem=recv_sem2,
            device_id={"tm": there},
            device_id_type=MESH,
        ).start()
    own_out = pltpu.make_async_copy(result.at[me], out_hbm.at[:, column_of], recv_sem2)
    own_out.start()
    sent = got.at[pl.ds(0, n - 1)]
    pltpu.make_async_copy(sent, sent, send_sem).wait()
    sent = result.at[pl.ds(0, nblocks - 1)]
    pltpu.make_async_copy(sent, sent, send_sem2).wait()
    pltpu.make_async_copy(out_hbm, out_hbm, recv_sem2).wait()


def shards(
    observations, outage_mask, group_length, prior_mean, transition, filter_gain, smoother_gain
):
    cap = observations.shape[0]
    nblocks, width, _ = transition.shape
    n = lax.axis_size("tm")
    chunks = n * cap * 3 // 4 // WORD
    reach = max([1] + [(r - 1) * s for r, s in zip(radices_of(chunks), strides_of(chunks))])
    tall = chunks + -(-reach // 8) * 8
    hbm = pl.BlockSpec(memory_space=pltpu.HBM)
    f32 = jnp.float32
    return pl.pallas_call(
        functools.partial(kernel, n),
        out_shape=jax.ShapeDtypeStruct(observations.shape, f32),
        in_specs=[hbm] * 7,
        out_specs=pl.BlockSpec(memory_space=pl.ANY),
        scratch_shapes=[
            pltpu.SMEM((1,), jnp.int32),
            pltpu.VMEM((cap, nblocks), jnp.int32),
            pltpu.VMEM((1, nblocks * width), f32),
            pltpu.VMEM((cap, nblocks * width), f32),
            pltpu.VMEM((nblocks, 2 * cap, width), f32),
            pltpu.VMEM((n, 2 * cap, width), f32),
            pltpu.VMEM((width, width), f32),
            pltpu.VMEM((width, width), f32),
            pltpu.VMEM((width, width), f32),
            pltpu.VMEM((1 << WORD, width, width), f32),
            pltpu.VMEM((1 << WORD, width, width), f32),
            pltpu.VMEM((chunks, width), jnp.int32),
            pltpu.SMEM((chunks, width), jnp.int32),
            pltpu.VMEM((chunks, width), f32),
            pltpu.VMEM((chunks + 8, width), f32),
            pltpu.VMEM((WORD, tall, width), f32),
            pltpu.VMEM((WORD, tall, width), f32),
            pltpu.VMEM((n, cap, width), f32),
            pltpu.SemaphoreType.DMA((7,)),
            pltpu.SemaphoreType.DMA,
            pltpu.SemaphoreType.DMA,
            pltpu.SemaphoreType.DMA,
            pltpu.SemaphoreType.DMA,
            pltpu.SemaphoreType.DMA,
        ],
        compiler_params=pltpu.CompilerParams(
            collective_id=0, has_side_effects=True, vmem_limit_bytes=64 << 20
        ),
    )(
        group_length,
        outage_mask,
        observations,
        prior_mean.reshape(1, -1),
        transition,
        filter_gain,
        smoother_gain,
    )


def strides_of(chunks):
    strides, span = [], 1
    for radix in radices_of(chunks):
        strides.append(span)
        span *= radix
    return strides


def solution(mesh):
    placed = (
        P(("parts", "tm"), None),
        P(("parts", "tm"), None),
        P(("parts", "tm")),
        P("parts"),
        P(),
        P(),
        P(),
    )
    return jax.shard_map(
        shards, mesh=mesh, in_specs=placed, out_specs=P(("parts", "tm"), None), check_vma=False
    )
```

time: 28 us -> 23.1 us (0.83)
  local copies, waits for them, and re-layouts: 6.52 us -> 1.47 us
  Pallas kernels: 20.4 us -> 20.7 us
    unnamed x13 -> x1, local copies, waits for them, and re-layouts: 6.52 us -> 1.47 us
    pallas_call x1, Pallas kernels: 20.4 us -> 20.7 us  [shards(): pl.pallas_call(functools.partial(kernel, n), out_shape=jax.ShapeDtypeStru...]
where the time goes in v2:
time: 23.1 us; the launch traced here: 22.9 us
  Pallas kernels  20.7 us (90%)
  local copies, waits for them, and re-layouts  1.47 us (6%)
  between operations  0.66 us (3%)
    pallas_call x1, Pallas kernels, shards(): pl.pallas_call(functools.partial(kernel, n), out_shape=jax.ShapeDtypeStru...  20.7 us
    unnamed x1, local copies, waits for them, and re-layouts  1.47 us

profile of v2, /device:TPU:0, one launch (start us, length us, event | category | flops | bytes accessed | tf_op | source)
XLA Modules:
  0.0 22.9 jit_solution(9512595295180034572)
XLA Ops:
  0.7 20.7 %shard_map.73 = f32[8,2048]{1,0:T(8,128)} custom-call(s32[1]{0:T(128)S(6)} %copy.9.length_hbm, s32[8,16]{1,0:T(8,128)} %mask_hbm.1, f32[8,2048]{1,0:T(8,128)} %obs_hbm.1, f32[1,2048]{1,0:T(1,128)} %bitcast.1, f32[16,128,128]{2,1,0:T(8,128)} %trans_hbm.1, f32[16,128,128]{2,1,0:T(8,128)} %filt_hbm.1, f32[16,128,128]{2,1,0:T(8,128)} %smooth_hbm.1), custom_call_target="tpu_custom_call" | custom-call | tf_op jit(solution)/shard_map/pallas_call | solution.py:345
  21.4 1.5 %copy.10 = f32[8,2048]{1,0:T(8,128)} copy(f32[8,2048]{1,0:T(8,128)} %shard_map.73) | data formatting | bytes 131072

commit v3 on v2

--- a/solution.py
+++ b/solution.py
@@ -7,21 +7,35 @@
 from jax.experimental.pallas import tpu as pltpu
 from jax.sharding import PartitionSpec as P
 
-highest = lax.Precision.HIGHEST
 MESH = pl.DeviceIdType.MESH
 WORD = 3
 
 
+def split(value):
+    high = value.astype(jnp.bfloat16)
+    return high, (value - high.astype(jnp.float32)).astype(jnp.bfloat16)
+
+
 def ready(weight):
-    return weight
+    high, low = split(weight)
+    return jnp.concatenate([high, high, low], axis=0)
 
 
 def mm(left, right):
-    return jnp.dot(left, right, precision=highest, preferred_element_type=jnp.float32)
+    high, low = split(left)
+    return jnp.dot(
+        jnp.concatenate([high, low, high], axis=1), right, preferred_element_type=jnp.float32
+    )
 
 
 def choose(chosen, values):
-    return jnp.dot(chosen, values, precision=highest, preferred_element_type=jnp.float32)
+    high, low = split(values)
+    chosen = chosen.astype(jnp.bfloat16)
+    return jnp.dot(
+        jnp.concatenate([chosen, chosen], axis=1),
+        jnp.concatenate([high, low], axis=0),
+        preferred_element_type=jnp.float32,
+    )
 
 
 def radices_of(chunks):
@@ -40,7 +54,7 @@
 
 def kernel(
     n,
-    length_hbm,
+    length_ref,
     mask_hbm,
     obs_hbm,
     prior_hbm,
@@ -48,7 +62,6 @@
     filt_hbm,
     smooth_hbm,
     out_hbm,
-    length_s,
     mask_v,
     prior_v,
     obs_v,
@@ -89,7 +102,6 @@
     loads = []
     for place, (source, target) in enumerate(
         (
-            (length_hbm, length_s),
             (mask_hbm, mask_v),
             (obs_hbm, obs_v),
             (trans_hbm.at[block], trans_v),
@@ -109,8 +121,7 @@
         )
 
     loads[0].wait()
-    loads[1].wait()
-    length = length_s[0]
+    length = length_ref[0]
     alive_here = (iota((cap, width), 0) < length).astype(jnp.float32)
     lane = iota((cap, width), 1)
     left_half = lane < half
@@ -120,7 +131,7 @@
     for b in range(nblocks):
         seen = jnp.broadcast_to(mask_f[:, b : b + 1], (cap, width))
         stage[b, cap : 2 * cap, :] = jnp.where(left_half, seen * alive_here, alive_lanes)
-    loads[2].wait()
+    loads[1].wait()
     for b in range(nblocks):
         stage[b, 0:cap, :] = obs_v[:, b * width : (b + 1) * width]
 
@@ -138,7 +149,7 @@
     own_in = pltpu.make_async_copy(stage.at[block], got.at[me], recv_sem)
     own_in.start()
 
-    for load in loads[3:]:
+    for load in loads[2:]:
         load.wait()
     trans = trans_v[...]
     gain = filt_v[...]
@@ -293,7 +304,7 @@
 
     columns = [jnp.concatenate(filtered, axis=0)] + ahead_of(buf_a, filtered, WORD, 1)
     total = mm(jnp.concatenate(columns, axis=1), levels[0])
-    finish = mm(jnp.broadcast_to(newest, (8, width)), levels[1])[0:1]
+    finish = mm(jnp.broadcast_to(newest, (16, width)), levels[1])[0:1]
     is_end = iota((chunks, width), 0) == chunks - 1
     total = total + jnp.concatenate(
         [
@@ -344,11 +355,10 @@
     f32 = jnp.float32
     return pl.pallas_call(
         functools.partial(kernel, n),
-        out_shape=jax.ShapeDtypeStruct(observations.shape, f32),
-        in_specs=[hbm] * 7,
+        out_shape=pltpu.VMEM(observations.shape, f32),
+        in_specs=[pl.BlockSpec(memory_space=pltpu.SMEM)] + [hbm] * 6,
         out_specs=pl.BlockSpec(memory_space=pl.ANY),
         scratch_shapes=[
-            pltpu.SMEM((1,), jnp.int32),
             pltpu.VMEM((cap, nblocks), jnp.int32),
             pltpu.VMEM((1, nblocks * width), f32),
             pltpu.VMEM((cap, nblocks * width), f32),
@@ -366,7 +376,7 @@
             pltpu.VMEM((WORD, tall, width), f32),
             pltpu.VMEM((WORD, tall, width), f32),
             pltpu.VMEM((n, cap, width), f32),
-            pltpu.SemaphoreType.DMA((7,)),
+            pltpu.SemaphoreType.DMA((6,)),
             pltpu.SemaphoreType.DMA,
             pltpu.SemaphoreType.DMA,
             pltpu.SemaphoreType.DMA,
@@ -374,16 +384,21 @@
             pltpu.SemaphoreType.DMA,
         ],
         compiler_params=pltpu.CompilerParams(
-            collective_id=0, has_side_effects=True, vmem_limit_bytes=64 << 20
+            collective_id=0, has_side_effects=True, vmem_limit_bytes=48 << 20
         ),
     )(
         group_length,
-        outage_mask,
-        observations,
-        prior_mean.reshape(1, -1),
-        transition,
-        filter_gain,
-        smoother_gain,
+        *(
+            pltpu.with_memory_space_constraint(value, pltpu.HBM)
+            for value in (
+                outage_mask,
+                observations,
+                prior_mean.reshape(1, -1),
+                transition,
+                filter_gain,
+                smoother_gain,
+            )
+        )
     )
 
 

time: 23.1 us -> 21 us (0.909)
  Pallas kernels: 20.7 us -> 19.5 us
  local copies, waits for them, and re-layouts: 1.47 us -> 0.63 us
    pallas_call x1, Pallas kernels: 20.7 us -> 19.5 us  [shards(): pl.pallas_call(functools.partial(kernel, n), out_shape=pltpu.VMEM(observa...]
    unnamed x1, local copies, waits for them, and re-layouts: 1.47 us -> 0.63 us
where the time goes in v3:
time: 21 us; the launch traced here: 20.8 us
  Pallas kernels  19.5 us (93%)
  between operations  0.66 us (3%)
  local copies, waits for them, and re-layouts  0.63 us (3%)
    pallas_call x1, Pallas kernels, shards(): pl.pallas_call(functools.partial(kernel, n), out_shape=pltpu.VMEM(observa...  19.5 us
    unnamed x1, local copies, waits for them, and re-layouts  0.63 us

profile of v3, /device:TPU:0, one launch (start us, length us, event | category | flops | bytes accessed | tf_op | source)
XLA Modules:
  0.0 20.8 jit_solution(17849714729326472231)
XLA Ops:
  0.7 19.5 %shard_map.73 = f32[8,2048]{1,0:T(8,128)S(1)} custom-call(s32[1]{0:T(128)S(6)} %copy.10.length_ref, s32[8,16]{1,0:T(8,128)} %mask_hbm.1, f32[8,2048]{1,0:T(8,128)} %obs_hbm.1, f32[1,2048]{1,0:T(1,128)} %bitcast.1, f32[16,128,128]{2,1,0:T(8,128)} %trans_hbm.1, f32[16,128,128]{2,1,0:T(8,128)} %filt_hbm.1, f32[16,128,128]{2,1,0:T(8,128)} %smooth_hbm.1), custom_call_target="tpu_custom_call" | custom-call | tf_op jit(solution)/shard_map/pallas_call | solution.py:356
  20.2 0.6 %copy.9 = f32[8,2048]{1,0:T(8,128)} copy(f32[8,2048]{1,0:T(8,128)S(1)} %shard_map.73) | data formatting | bytes 131072

commit v4 on v0

v4 whole, which is shorter than its diff:
```python
import functools

import jax
import jax.numpy as jnp
from jax import lax
from jax.experimental import pallas as pl
from jax.experimental.pallas import tpu as pltpu
from jax.sharding import PartitionSpec as P

MESH = pl.DeviceIdType.MESH
WORD = 3
PER = 2


def split(value):
    high = value.astype(jnp.bfloat16)
    return high, (value - high.astype(jnp.float32)).astype(jnp.bfloat16)


def ready(weight):
    high, low = split(weight)
    return jnp.concatenate([high, high, low], axis=0)


def mm(left, right):
    high, low = split(left)
    return jnp.dot(
        jnp.concatenate([high, low, high], axis=1), right, preferred_element_type=jnp.float32
    )


def choose(chosen, values):
    high, low = split(values)
    chosen = chosen.astype(jnp.bfloat16)
    return jnp.dot(
        jnp.concatenate([chosen, chosen], axis=1),
        jnp.concatenate([high, low], axis=0),
        preferred_element_type=jnp.float32,
    )


def radices_of(chunks):
    found, span = [], 1
    for radix in (6, 6, 4, 4, 4, 4):
        if span >= chunks:
            break
        found.append(radix)
        span *= radix
    return found


def iota(shape, axis):
    return lax.broadcasted_iota(jnp.int32, shape, axis)


def kernel(
    n,
    length_ref,
    mask_hbm,
    obs_hbm,
    prior_hbm,
    trans_hbm,
    filt_hbm,
    smooth_hbm,
    out_hbm,
    alive_v,
    got_obs,
    got_mask,
    got_alive,
    prior_v,
    trans_v,
    filt_v,
    smooth_v,
    words,
    words_t,
    index_v,
    index_s,
    offsets,
    entries,
    buf_a,
    buf_b,
    result,
    load_sem,
    send_sem,
    recv_sem,
    out_sem,
    index_sem,
):
    cap, both = got_obs.shape[1:]
    width = trans_v.shape[1]
    nblocks = trans_hbm.shape[0]
    owners = nblocks // PER
    slots = n * cap
    live = slots * 3 // 4
    chunks = live // WORD
    padded = -(-live // width) * width

    me = lax.axis_index("tm")
    is_owner = me < owners
    block = me * PER
    mine = range(PER)

    def own_columns():
        return pl.ds(pl.multiple_of(me * both, both), both)

    loads = [
        pltpu.make_async_copy(source, target, load_sem.at[place])
        for place, (source, target) in enumerate(
            (
                (trans_hbm.at[pl.ds(block, PER)], trans_v),
                (filt_hbm.at[pl.ds(block, PER)], filt_v),
                (smooth_hbm.at[pl.ds(block, PER)], smooth_v),
                (prior_hbm, prior_v),
            )
        )
    ]

    barrier = pltpu.get_barrier_semaphore()

    def greet(there):
        pl.semaphore_signal(barrier, inc=1, device_id={"tm": there}, device_id_type=MESH)

    @pl.when(is_owner)
    def _():
        for load in loads:
            load.start()
        for step in range(1, n):
            greet(lax.rem(me + step, n))

    @pl.when(jnp.logical_not(is_owner))
    def _():
        for owner in range(owners):
            greet(owner)

    length = length_ref[0]
    own_slot = iota((cap, width), 0) * width + iota((cap, width), 1) - me * cap
    alive_v[...] = ((own_slot >= 0) & (own_slot < length)).astype(jnp.float32)

    @pl.when(is_owner)
    def _():
        pl.semaphore_wait(barrier, n - 1)

    @pl.when(jnp.logical_not(is_owner))
    def _():
        pl.semaphore_wait(barrier, owners)

    for owner in range(owners):
        parcels = (
            (alive_v, got_alive.at[me]),
            (mask_hbm, got_mask.at[me]),
            (obs_hbm.at[:, owner * both : (owner + 1) * both], got_obs.at[me]),
        )

        @pl.when(me != owner)
        def _():
            for kind, (source, target) in enumerate(parcels):
                pltpu.make_async_remote_copy(
                    src_ref=source,
                    dst_ref=target,
                    send_sem=send_sem.at[kind],
                    recv_sem=recv_sem.at[kind],
                    device_id={"tm": owner},
                    device_id_type=MESH,
                ).start()

        @pl.when(me == owner)
        def _():
            for kind, (source, target) in enumerate(parcels):
                pltpu.make_async_copy(source, target, recv_sem.at[kind]).start()

    @pl.when(is_owner)
    def _():
        for load in loads:
            load.wait()
        trans = [trans_v[j] for j in mine]
        gain = [filt_v[j] for j in mine]
        trans_t = [trans[j].T for j in mine]
        update = [trans[j] - mm(gain[j], ready(trans[j])) for j in mine]
        update_t = [update[j].T for j in mine]
        gain_t = [ready(gain[j].T) for j in mine]
        step_t = [ready(jnp.concatenate([update_t[j], trans_t[j]], axis=1)) for j in mine]

        def tile(whole, row, column):
            return whole[row * width : (row + 1) * width, column * width : (column + 1) * width]

        for j in mine:
            rows = jnp.concatenate([trans[j], update[j]], axis=0)
            square = mm(rows, ready(jnp.concatenate([trans[j], update[j]], axis=1)))
            square_t = mm(jnp.concatenate([trans_t[j], update_t[j]], axis=0), step_t[j])
            pairs = [tile(square, hi, lo) for hi in range(2) for lo in range(2)]
            pairs_t = [tile(square_t, lo, 1 - hi) for hi in range(2) for lo in range(2)]
            cube = mm(rows, ready(jnp.concatenate(pairs, axis=1)))
            cube_t = mm(jnp.concatenate(pairs_t, axis=0), step_t[j])
            for last in range(2):
                for p in range(4):
                    words[8 * j + 4 * last + p] = tile(cube, last, p)
                    words_t[8 * j + 4 * last + p] = tile(cube_t, p, 1 - last)

        for kind, got in enumerate((got_alive, got_mask, got_obs)):
            pltpu.make_async_copy(got, got, recv_sem.at[kind]).wait()
        readings = got_obs[...].reshape(slots, both)
        gained_slot = [
            mm(readings[:, j * width : (j + 1) * width], gain_t[j]) for j in mine
        ]
        alive_sum = jnp.sum(got_alive[...], axis=0)
        alive_row = jnp.concatenate(
            [alive_sum[k : k + 1] for k in range(slots // width)], axis=1
        )
        earlier = (iota((slots, slots), 0) < iota((slots, slots), 1)).astype(jnp.bfloat16)
        place = jnp.dot(
            jnp.broadcast_to(alive_row, (16, slots)).astype(jnp.bfloat16),
            earlier,
            preferred_element_type=jnp.float32,
        )[0:1]
        place = jnp.where(alive_row > 0.5, place, -1.0)
        mask = got_mask[...].reshape(slots, nblocks).astype(jnp.float32).astype(jnp.bfloat16)
        which = jnp.concatenate(
            [(iota((nblocks, width), 0) == block + j).astype(jnp.bfloat16) for j in mine], axis=1
        )
        seen_slot = jnp.dot(mask, which, preferred_element_type=jnp.float32)
        row = iota((padded, slots), 0)
        within = sum((row >= s * chunks).astype(jnp.int32) for s in range(1, WORD))
        step_of = WORD * (row - within * chunks) + within
        step_of = jnp.where(row < live, step_of, -2).astype(jnp.float32)
        gather = (jnp.broadcast_to(place, (padded, slots)) == step_of).astype(jnp.float32)
        seen_rows = jnp.dot(
            gather.astype(jnp.bfloat16),
            seen_slot.astype(jnp.bfloat16),
            preferred_element_type=jnp.float32,
        )

        def by_step(rows):
            return [rows[s * chunks : (s + 1) * chunks] for s in range(WORD)]

        seen = [
            [part > 0.5 for part in by_step(seen_rows[:, j * width : (j + 1) * width])]
            for j in mine
        ]
        for j in mine:
            index_v[j] = sum(jnp.where(seen[j][s], 1 << s, 0) for s in range(WORD))
        index_copy = pltpu.make_async_copy(index_v, index_s, index_sem)
        index_copy.start()
        gain_rows = choose(gather, jnp.concatenate(gained_slot, axis=1))
        gains = [
            [
                jnp.where(seen[j][s], part, 0.0)
                for s, part in enumerate(by_step(gain_rows[:, j * width : (j + 1) * width]))
            ]
            for j in mine
        ]

        def advance(j, state, s):
            moved = mm(state, step_t[j])
            return jnp.where(seen[j][s], moved[:, :width], moved[:, width:]) + gains[j][s]

        offset = [gains[j][0] for j in mine]
        for s in range(1, WORD):
            offset = [advance(j, offset[j], s) for j in mine]
        for j in mine:
            offsets[j] = offset[j]
        index_copy.wait()

        radices = [WORD] + radices_of(chunks)

        def powers_by_steps(j, levels):
            base = smooth_v[j].T
            for level, radix in enumerate(radices):
                wanted = radix - 1 if level == len(radices) - 1 else radix
                powers = [base]
                while len(powers) < wanted:
                    take = min(len(powers), wanted - len(powers))
                    more = mm(powers[-1], ready(jnp.concatenate(powers[:take], axis=1)))
                    powers += [more[:, i * width : (i + 1) * width] for i in range(take)]
                    yield
                if level == 0:
                    ends = mm(trans_t[j], ready(jnp.concatenate(powers, axis=1)))
                    yield
                    ends = [ends[:, i * width : (i + 1) * width] for i in range(radix)]
                    eye_f = (iota((width, width), 0) == iota((width, width), 1)).astype(
                        jnp.float32
                    )
                    starts = [l - e for l, e in zip([eye_f] + powers[: radix - 1], ends)]
                    levels.append(ready(jnp.concatenate(starts, axis=0)))
                    levels.append(ready(jnp.concatenate(ends, axis=1)))
                else:
                    levels.append(ready(jnp.concatenate(powers[: radix - 1], axis=0)))
                base = powers[-1]

        levels = [[] for j in mine]
        side = [powers_by_steps(j, levels[j]) for j in mine]

        eye = iota((width, width), 0) == iota((width, width), 1)
        state = [
            prior_v[:, pl.ds(pl.multiple_of((block + j) * width, width), width)] for j in mine
        ]
        for j in mine:
            entries[j, 0:1, :] = state[j]
        for c in range(0, chunks, 2):
            column = [None] * PER
            for j in mine:
                terms = words[8 * j + index_s[j, c, 0]] * state[j]
                terms = terms + jnp.where(eye, offsets[j, c : c + 1, :], 0.0)
                column[j] = jnp.sum(terms, axis=1, keepdims=True)
            for j in mine:
                entries[j, c + 1 : c + 2, :] = jnp.sum(
                    jnp.where(eye, column[j], 0.0), axis=0, keepdims=True
                )
                terms = words_t[8 * j + index_s[j, c + 1, 0]] * column[j]
                state[j] = jnp.sum(terms, axis=0, keepdims=True) + offsets[j, c + 1 : c + 2, :]
                entries[j, c + 2 : c + 3, :] = state[j]
                next(side[j], None)
        for j in mine:
            for _ in side[j]:
                pass

        state = [entries[j, 0:chunks, :] for j in mine]
        filtered = [[] for j in mine]
        for s in range(WORD - 1):
            for j in mine:
                state[j] = advance(j, state[j], s)
                filtered[j].append(state[j])
        for j in mine:
            filtered[j].append(entries[j, 1 : chunks + 1, :])

        tail = buf_a.shape[2] - chunks
        for j in mine:
            for s in range(WORD):
                buf_a[j, s, chunks:, :] = jnp.zeros((tail, width), jnp.float32)
                buf_b[j, s, chunks:, :] = jnp.zeros((tail, width), jnp.float32)

        def ahead_of(buf, j, values, radix, stride):
            for s in range(WORD):
                buf[j, s, 0:chunks, :] = values[s]
            columns = []
            for i in range(1, radix):
                parts = []
                for s in range(WORD):
                    later = s + i * stride
                    first = later // WORD
                    parts.append(buf[j, later % WORD, first : first + chunks, :])
                columns.append(jnp.concatenate(parts, axis=0))
            return columns

        total = [None] * PER
        for j in mine:
            columns = [jnp.concatenate(filtered[j], axis=0)]
            columns += ahead_of(buf_a, j, filtered[j], WORD, 1)
            total[j] = mm(jnp.concatenate(columns, axis=1), levels[j][0])
            newest = jnp.broadcast_to(entries[j, chunks : chunks + 1, :], (16, width))
            finish = mm(newest, levels[j][1])[0:1]
            is_end = iota((chunks, width), 0) == chunks - 1
            total[j] = total[j] + jnp.concatenate(
                [
                    jnp.where(is_end, finish[:, i * width : (i + 1) * width], 0.0)
                    for i in reversed(range(WORD))
                ],
                axis=0,
            )
        stride = WORD
        for level, radix in enumerate(radices[1:]):
            buf = buf_b if level % 2 == 0 else buf_a
            for j in mine:
                columns = ahead_of(buf, j, by_step(total[j]), radix, stride)
                total[j] = total[j] + mm(
                    jnp.concatenate(columns, axis=1), levels[j][level + 2]
                )
            stride *= radix

        spread = gather.T[:, :live]
        result[...] = choose(spread, jnp.concatenate(total, axis=1)).reshape(n, cap, both)

        for there in range(n):

            @pl.when(me != there)
            def _():
                pltpu.make_async_remote_copy(
                    src_ref=result.at[there],
                    dst_ref=out_hbm.at[:, own_columns()],
                    send_sem=send_sem.at[3],
                    recv_sem=out_sem,
                    device_id={"tm": there},
                    device_id_type=MESH,
                ).start()

            @pl.when(me == there)
            def _():
                pltpu.make_async_copy(
                    result.at[there], out_hbm.at[:, own_columns()], out_sem
                ).start()

        for kind, got in enumerate((got_alive, got_mask, got_obs)):
            sent = got.at[pl.ds(0, owners - 1)]
            pltpu.make_async_copy(sent, sent, send_sem.at[kind]).wait()
        sent = result.at[pl.ds(0, n - 1)]
        pltpu.make_async_copy(sent, sent, send_sem.at[3]).wait()

    @pl.when(jnp.logical_not(is_owner))
    def _():
        for kind, got in enumerate((got_alive, got_mask, got_obs)):
            sent = got.at[pl.ds(0, owners)]
            pltpu.make_async_copy(sent, sent, send_sem.at[kind]).wait()

    pltpu.make_async_copy(out_hbm, out_hbm, out_sem).wait()


def shards(
    observations, outage_mask, group_length, prior_mean, transition, filter_gain, smoother_gain
):
    cap = observations.shape[0]
    nblocks, width, _ = transition.shape
    n = lax.axis_size("tm")
    chunks = n * cap * 3 // 4 // WORD
    reach = max([1] + [(r - 1) * s for r, s in zip(radices_of(chunks), strides_of(chunks))])
    tall = chunks + -(-reach // 8) * 8
    hbm = pl.BlockSpec(memory_space=pltpu.HBM)
    f32 = jnp.float32
    return pl.pallas_call(
        functools.partial(kernel, n),
        out_shape=pltpu.VMEM(observations.shape, f32),
        in_specs=[pl.BlockSpec(memory_space=pltpu.SMEM)] + [hbm] * 6,
        out_specs=pl.BlockSpec(memory_space=pl.ANY),
        scratch_shapes=[
            pltpu.VMEM((cap, width), f32),
            pltpu.VMEM((n, cap, PER * width), f32),
            pltpu.VMEM((n, cap, nblocks), jnp.int32),
            pltpu.VMEM((n, cap, width), f32),
            pltpu.VMEM((1, nblocks * width), f32),
            pltpu.VMEM((PER, width, width), f32),
            pltpu.VMEM((PER, width, width), f32),
            pltpu.VMEM((PER, width, width), f32),
            pltpu.VMEM((PER << WORD, width, width), f32),
            pltpu.VMEM((PER << WORD, width, width), f32),
            pltpu.VMEM((PER, chunks, width), jnp.int32),
            pltpu.SMEM((PER, chunks, width), jnp.int32),
            pltpu.VMEM((PER, chunks, width), f32),
            pltpu.VMEM((PER, chunks + 8, width), f32),
            pltpu.VMEM((PER, WORD, tall, width), f32),
            pltpu.VMEM((PER, WORD, tall, width), f32),
            pltpu.VMEM((n, cap, PER * width), f32),
            pltpu.SemaphoreType.DMA((4,)),
            pltpu.SemaphoreType.DMA((4,)),
            pltpu.SemaphoreType.DMA((3,)),
            pltpu.SemaphoreType.DMA,
            pltpu.SemaphoreType.DMA,
        ],
        compiler_params=pltpu.CompilerParams(
            collective_id=0, has_side_effects=True, vmem_limit_bytes=48 << 20
        ),
    )(
        group_length,
        *(
            pltpu.with_memory_space_constraint(value, pltpu.HBM)
            for value in (
                outage_mask,
                observations,
                prior_mean.reshape(1, -1),
                transition,
                filter_gain,
                smoother_gain,
            )
        )
    )


def strides_of(chunks):
    strides, span = [], 1
    for radix in radices_of(chunks):
        strides.append(span)
        span *= radix
    return strides


def solution(mesh):
    placed = (
        P(("parts", "tm"), None),
        P(("parts", "tm"), None),
        P(("parts", "tm")),
        P("parts"),
        P(),
        P(),
        P(),
    )
    return jax.shard_map(
        shards, mesh=mesh, in_specs=placed, out_specs=P(("parts", "tm"), None), check_vma=False
    )
```

time: 489 us -> 21.6 us (0.04)
  matrix products: 184 us -> 0 us
  blocking collectives: 122 us -> 0 us
  waiting for transfers between devices: 95.8 us -> 0 us
  other arithmetic: 39.1 us -> 0 us
  local copies, waits for them, and re-layouts: 29.8 us -> 0.63 us
  Pallas kernels: 0 us -> 20.1 us
  between operations: 14.3 us -> 0.66 us
    dot_general x82 -> x0, matrix products: 184 us -> none  [the longest x64 149 us: mat_vec(): return jnp.einsum('bij,bj->bi', matrix, vector, precision=highest)]
    all_gather x2 -> x0, blocking collectives: 122 us -> none  [carried_in(): gathered = jax.tree.map(lambda a: lax.all_gather(a, axis), part)]
    all_gather x2 -> x0, waiting for transfers between devices: 95.8 us -> none  [carried_in(): gathered = jax.tree.map(lambda a: lax.all_gather(a, axis), part)]
    dynamic_slice x56 -> x0, local copies, waits for them, and re-layouts: 26.4 us -> none  [the longest x40 26.3 us: shards(): lax.scan(forward, entry_state, (step_mats, gain_terms, alive_slot))]
    select_n x17 -> x0, other arithmetic: 21.8 us -> none  [the longest x16 16.5 us: backward(): next_state = jnp.where(is_alive, result, later_state)]
    pallas_call x0 -> x1, Pallas kernels: none -> 20.1 us  [shards(): pl.pallas_call(functools.partial(kernel, n), out_shape=pltpu.VMEM(observa...]
    dynamic_update_slice x16 -> x0, other arithmetic: 16.3 us -> none  [shards(): lax.scan(forward, entry_state, (step_mats, gain_terms, alive_slot))]
  transfers between devices with their start and end apart: 2 -> 0, of which waited for: 1 -> 0; matrix products, arithmetic and copies ran while one was open for 20% -> 0% of each run, Pallas kernels for 0% -> 0%
where the time goes in v4:
time: 21.6 us; the launch traced here: 21.4 us
  Pallas kernels  20.1 us (93%)
  between operations  0.66 us (3%)
  local copies, waits for them, and re-layouts  0.63 us (3%)
    pallas_call x1, Pallas kernels, shards(): pl.pallas_call(functools.partial(kernel, n), out_shape=pltpu.VMEM(observa...  20.1 us
    unnamed x1, local copies, waits for them, and re-layouts  0.63 us

profile of v4, /device:TPU:0, one launch (start us, length us, event | category | flops | bytes accessed | tf_op | source)
XLA Modules:
  0.0 21.4 jit_solution(12082619718052273593)
XLA Ops:
  0.7 20.1 %shard_map.73 = f32[8,2048]{1,0:T(8,128)S(1)} custom-call(s32[1]{0:T(128)S(6)} %copy.10.length_ref, s32[8,16]{1,0:T(8,128)} %mask_hbm.1, f32[8,2048]{1,0:T(8,128)} %obs_hbm.1, f32[1,2048]{1,0:T(1,128)} %bitcast.1, f32[16,128,128]{2,1,0:T(8,128)} %trans_hbm.1, f32[16,128,128]{2,1,0:T(8,128)} %filt_hbm.1, f32[16,128,128]{2,1,0:T(8,128)} %smooth_hbm.1), custom_call_target="tpu_custom_call" | custom-call | tf_op jit(solution)/shard_map/pallas_call | solution.py:417
  20.8 0.6 %copy.9 = f32[8,2048]{1,0:T(8,128)} copy(f32[8,2048]{1,0:T(8,128)S(1)} %shard_map.73) | data formatting | bytes 131072

commit v5 on v4

--- a/solution.py
+++ b/solution.py
@@ -47,6 +47,14 @@
         found.append(radix)
         span *= radix
     return found
+
+
+def phases_of(n, cap, live, chunks):
+    found = []
+    for known in (n // 2, n - n // 4):
+        sure = (live - (n - known) * cap) // WORD // 4 * 4
+        found.append((known, sure))
+    return found + [(n, chunks)]
 
 
 def iota(shape, axis):
@@ -75,7 +83,6 @@
     words_t,
     index_v,
     index_s,
-    offsets,
     entries,
     buf_a,
     buf_b,
@@ -144,6 +151,8 @@
     def _():
         pl.semaphore_wait(barrier, owners)
 
+    ends = [known for known, _ in phases_of(n, cap, live, chunks)]
+    my_phase = sum((me >= known).astype(jnp.int32) for known in ends[:-1])
     for owner in range(owners):
         parcels = (
             (alive_v, got_alive.at[me]),
@@ -158,7 +167,7 @@
                     src_ref=source,
                     dst_ref=target,
                     send_sem=send_sem.at[kind],
-                    recv_sem=recv_sem.at[kind],
+                    recv_sem=recv_sem.at[3 * my_phase + kind],
                     device_id={"tm": owner},
                     device_id_type=MESH,
                 ).start()
@@ -166,7 +175,9 @@
         @pl.when(me == owner)
         def _():
             for kind, (source, target) in enumerate(parcels):
-                pltpu.make_async_copy(source, target, recv_sem.at[kind]).start()
+                pltpu.make_async_copy(
+                    source, target, recv_sem.at[3 * my_phase + kind]
+                ).start()
 
     @pl.when(is_owner)
     def _():
@@ -196,69 +207,8 @@
                     words[8 * j + 4 * last + p] = tile(cube, last, p)
                     words_t[8 * j + 4 * last + p] = tile(cube_t, p, 1 - last)
 
-        for kind, got in enumerate((got_alive, got_mask, got_obs)):
-            pltpu.make_async_copy(got, got, recv_sem.at[kind]).wait()
-        readings = got_obs[...].reshape(slots, both)
-        gained_slot = [
-            mm(readings[:, j * width : (j + 1) * width], gain_t[j]) for j in mine
-        ]
-        alive_sum = jnp.sum(got_alive[...], axis=0)
-        alive_row = jnp.concatenate(
-            [alive_sum[k : k + 1] for k in range(slots // width)], axis=1
-        )
-        earlier = (iota((slots, slots), 0) < iota((slots, slots), 1)).astype(jnp.bfloat16)
-        place = jnp.dot(
-            jnp.broadcast_to(alive_row, (16, slots)).astype(jnp.bfloat16),
-            earlier,
-            preferred_element_type=jnp.float32,
-        )[0:1]
-        place = jnp.where(alive_row > 0.5, place, -1.0)
-        mask = got_mask[...].reshape(slots, nblocks).astype(jnp.float32).astype(jnp.bfloat16)
-        which = jnp.concatenate(
-            [(iota((nblocks, width), 0) == block + j).astype(jnp.bfloat16) for j in mine], axis=1
-        )
-        seen_slot = jnp.dot(mask, which, preferred_element_type=jnp.float32)
-        row = iota((padded, slots), 0)
-        within = sum((row >= s * chunks).astype(jnp.int32) for s in range(1, WORD))
-        step_of = WORD * (row - within * chunks) + within
-        step_of = jnp.where(row < live, step_of, -2).astype(jnp.float32)
-        gather = (jnp.broadcast_to(place, (padded, slots)) == step_of).astype(jnp.float32)
-        seen_rows = jnp.dot(
-            gather.astype(jnp.bfloat16),
-            seen_slot.astype(jnp.bfloat16),
-            preferred_element_type=jnp.float32,
-        )
-
-        def by_step(rows):
-            return [rows[s * chunks : (s + 1) * chunks] for s in range(WORD)]
-
-        seen = [
-            [part > 0.5 for part in by_step(seen_rows[:, j * width : (j + 1) * width])]
-            for j in mine
-        ]
-        for j in mine:
-            index_v[j] = sum(jnp.where(seen[j][s], 1 << s, 0) for s in range(WORD))
-        index_copy = pltpu.make_async_copy(index_v, index_s, index_sem)
-        index_copy.start()
-        gain_rows = choose(gather, jnp.concatenate(gained_slot, axis=1))
-        gains = [
-            [
-                jnp.where(seen[j][s], part, 0.0)
-                for s, part in enumerate(by_step(gain_rows[:, j * width : (j + 1) * width]))
-            ]
-            for j in mine
-        ]
-
-        def advance(j, state, s):
-            moved = mm(state, step_t[j])
-            return jnp.where(seen[j][s], moved[:, :width], moved[:, width:]) + gains[j][s]
-
-        offset = [gains[j][0] for j in mine]
-        for s in range(1, WORD):
-            offset = [advance(j, offset[j], s) for j in mine]
-        for j in mine:
-            offsets[j] = offset[j]
-        index_copy.wait()
+        def by_step(rows, count):
+            return [rows[s * count : (s + 1) * count] for s in range(WORD)]
 
         radices = [WORD] + radices_of(chunks)
 
@@ -288,39 +238,132 @@
 
         levels = [[] for j in mine]
         side = [powers_by_steps(j, levels[j]) for j in mine]
-
         eye = iota((width, width), 0) == iota((width, width), 1)
         state = [
             prior_v[:, pl.ds(pl.multiple_of((block + j) * width, width), width)] for j in mine
         ]
         for j in mine:
             entries[j, 0:1, :] = state[j]
-        for c in range(0, chunks, 2):
-            column = [None] * PER
+        earlier = (iota((slots, slots), 0) < iota((slots, slots), 1)).astype(jnp.bfloat16)
+        which = jnp.concatenate(
+            [(iota((nblocks, width), 0) == block + j).astype(jnp.bfloat16) for j in mine], axis=1
+        )
+        alive_sum = jnp.zeros((cap, width), jnp.float32)
+        gained_slot = [[] for j in mine]
+        seen_slot = []
+        filtered = [[[] for s in range(WORD)] for j in mine]
+
+        first_device, first = 0, 0
+        for phase, (known, until) in enumerate(phases_of(n, cap, live, chunks)):
+            count = until - first
+            for kind, got in enumerate((got_alive, got_mask, got_obs)):
+                part = got.at[pl.ds(first_device, known - first_device)]
+                pltpu.make_async_copy(part, part, recv_sem.at[3 * phase + kind]).wait()
+            fresh = (known - first_device) * cap
+            here = known * cap
+            readings = got_obs[first_device:known].reshape(fresh, both)
             for j in mine:
-                terms = words[8 * j + index_s[j, c, 0]] * state[j]
-                terms = terms + jnp.where(eye, offsets[j, c : c + 1, :], 0.0)
-                column[j] = jnp.sum(terms, axis=1, keepdims=True)
+                gained_slot[j].append(
+                    mm(readings[:, j * width : (j + 1) * width], gain_t[j])
+                )
+            mask = got_mask[first_device:known].reshape(fresh, nblocks)
+            mask = mask.astype(jnp.float32).astype(jnp.bfloat16)
+            seen_slot.append(jnp.dot(mask, which, preferred_element_type=jnp.float32))
+            alive_sum = alive_sum + jnp.sum(got_alive[first_device:known], axis=0)
+            alive_row = jnp.concatenate(
+                [alive_sum[k : k + 1] for k in range(slots // width)], axis=1
+            )
+            place = jnp.dot(
+                jnp.broadcast_to(alive_row, (16, slots)).astype(jnp.bfloat16),
+                earlier,
+                preferred_element_type=jnp.float32,
+            )[0:1]
+            place = jnp.where(alive_row > 0.5, place, -1.0)
+            rows = -(-WORD * count // 16) * 16
+            row = iota((rows, slots), 0)
+            within = sum((row >= s * count).astype(jnp.int32) for s in range(1, WORD))
+            step_of = WORD * (first + row - within * count) + within
+            step_of = jnp.where(row < WORD * count, step_of, -2).astype(jnp.float32)
+            gather = (jnp.broadcast_to(place, (rows, slots)) == step_of).astype(jnp.float32)
+            gather = gather[:, :here]
+            seen_rows = jnp.dot(
+                gather.astype(jnp.bfloat16),
+                jnp.concatenate(seen_slot, axis=0).astype(jnp.bfloat16),
+                preferred_element_type=jnp.float32,
+            )
+            seen = [
+                [part > 0.5 for part in by_step(seen_rows[:, j * width : (j + 1) * width], count)]
+                for j in mine
+            ]
+            index_v[phase] = jnp.zeros(index_v.shape[1:], jnp.int32)
             for j in mine:
-                entries[j, c + 1 : c + 2, :] = jnp.sum(
-                    jnp.where(eye, column[j], 0.0), axis=0, keepdims=True
+                index_v[phase, j, 0:count, :] = sum(
+                    jnp.where(seen[j][s], 1 << s, 0) for s in range(WORD)
                 )
-                terms = words_t[8 * j + index_s[j, c + 1, 0]] * column[j]
-                state[j] = jnp.sum(terms, axis=0, keepdims=True) + offsets[j, c + 1 : c + 2, :]
-                entries[j, c + 2 : c + 3, :] = state[j]
-                next(side[j], None)
+            index_copy = pltpu.make_async_copy(
+                index_v.at[phase], index_s.at[phase], index_sem.at[phase]
+            )
+            index_copy.start()
+            gain_rows = choose(
+                gather,
+                jnp.concatenate(
+                    [jnp.concatenate(gained_slot[j], axis=0) for j in mine], axis=1
+                ),
+            )
+            gains = [
+                [
+                    jnp.where(seen[j][s], part, 0.0)
+                    for s, part in enumerate(
+                        by_step(gain_rows[:, j * width : (j + 1) * width], count)
+                    )
+                ]
+                for j in mine
+            ]
+
+            def advance(j, value, s):
+                moved = mm(value, step_t[j])
+                return jnp.where(seen[j][s], moved[:, :width], moved[:, width:]) + gains[j][s]
+
+            offset = [gains[j][0] for j in mine]
+            for s in range(1, WORD):
+                offset = [advance(j, offset[j], s) for j in mine]
+            index_copy.wait()
+
+            for c in range(0, count, 2):
+                column = [None] * PER
+                for j in mine:
+                    terms = words[8 * j + index_s[phase, j, c, 0]] * state[j]
+                    terms = terms + jnp.where(eye, offset[j][c : c + 1, :], 0.0)
+                    column[j] = jnp.sum(terms, axis=1, keepdims=True)
+                for j in mine:
+                    at = first + c + 1
+                    entries[j, at : at + 1, :] = jnp.sum(
+                        jnp.where(eye, column[j], 0.0), axis=0, keepdims=True
+                    )
+                    terms = words_t[8 * j + index_s[phase, j, c + 1, 0]] * column[j]
+                    state[j] = jnp.sum(terms, axis=0, keepdims=True) + offset[j][c + 1 : c + 2, :]
+                    entries[j, at + 1 : at + 2, :] = state[j]
+                    next(side[j], None)
+
+            inner = [entries[j, first:until, :] for j in mine]
+            for s in range(WORD - 1):
+                for j in mine:
+                    inner[j] = advance(j, inner[j], s)
+                    filtered[j][s].append(inner[j])
+            for j in mine:
+                filtered[j][WORD - 1].append(entries[j, first + 1 : until + 1, :])
+            first_device, first = known, until
         for j in mine:
             for _ in side[j]:
                 pass
-
-        state = [entries[j, 0:chunks, :] for j in mine]
-        filtered = [[] for j in mine]
-        for s in range(WORD - 1):
-            for j in mine:
-                state[j] = advance(j, state[j], s)
-                filtered[j].append(state[j])
-        for j in mine:
-            filtered[j].append(entries[j, 1 : chunks + 1, :])
+        filtered = [[jnp.concatenate(parts, axis=0) for parts in filtered[j]] for j in mine]
+
+        place = jnp.broadcast_to(place, (padded, slots))
+        row = iota((padded, slots), 0)
+        within = sum((row >= s * chunks).astype(jnp.int32) for s in range(1, WORD))
+        step_of = WORD * (row - within * chunks) + within
+        step_of = jnp.where(row < live, step_of, -2).astype(jnp.float32)
+        spread = (place == step_of).astype(jnp.float32).T[:, :live]
 
         tail = buf_a.shape[2] - chunks
         for j in mine:
@@ -360,13 +403,12 @@
         for level, radix in enumerate(radices[1:]):
             buf = buf_b if level % 2 == 0 else buf_a
             for j in mine:
-                columns = ahead_of(buf, j, by_step(total[j]), radix, stride)
+                columns = ahead_of(buf, j, by_step(total[j], chunks), radix, stride)
                 total[j] = total[j] + mm(
                     jnp.concatenate(columns, axis=1), levels[j][level + 2]
                 )
             stride *= radix
 
-        spread = gather.T[:, :live]
         result[...] = choose(spread, jnp.concatenate(total, axis=1)).reshape(n, cap, both)
 
         for there in range(n):
@@ -430,18 +472,17 @@
             pltpu.VMEM((PER, width, width), f32),
             pltpu.VMEM((PER << WORD, width, width), f32),
             pltpu.VMEM((PER << WORD, width, width), f32),
-            pltpu.VMEM((PER, chunks, width), jnp.int32),
-            pltpu.SMEM((PER, chunks, width), jnp.int32),
-            pltpu.VMEM((PER, chunks, width), f32),
+            pltpu.VMEM((3, PER, chunks, width), jnp.int32),
+            pltpu.SMEM((3, PER, chunks, width), jnp.int32),
             pltpu.VMEM((PER, chunks + 8, width), f32),
             pltpu.VMEM((PER, WORD, tall, width), f32),
             pltpu.VMEM((PER, WORD, tall, width), f32),
             pltpu.VMEM((n, cap, PER * width), f32),
             pltpu.SemaphoreType.DMA((4,)),
             pltpu.SemaphoreType.DMA((4,)),
+            pltpu.SemaphoreType.DMA((9,)),
+            pltpu.SemaphoreType.DMA,
             pltpu.SemaphoreType.DMA((3,)),
-            pltpu.SemaphoreType.DMA,
-            pltpu.SemaphoreType.DMA,
         ],
         compiler_params=pltpu.CompilerParams(
             collective_id=0, has_side_effects=True, vmem_limit_bytes=48 << 20

time: 21.6 us -> 23 us (1.065)
  Pallas kernels: 20.1 us -> 21.6 us
    pallas_call x1, Pallas kernels: 20.1 us -> 21.6 us  [shards(): pl.pallas_call(functools.partial(kernel, n), out_shape=pltpu.VMEM(observa...]
where the time goes in v5:
time: 23 us; the launch traced here: 22.9 us
  Pallas kernels  21.6 us (94%)
  between operations  0.66 us (3%)
  local copies, waits for them, and re-layouts  0.63 us (3%)
    pallas_call x1, Pallas kernels, shards(): pl.pallas_call(functools.partial(kernel, n), out_shape=pltpu.VMEM(observa...  21.6 us
    unnamed x1, local copies, waits for them, and re-layouts  0.63 us

profile of v5, /device:TPU:0, one launch (start us, length us, event | category | flops | bytes accessed | tf_op | source)
XLA Modules:
  0.0 22.9 jit_solution(17186287909972847402)
XLA Ops:
  0.7 21.6 %shard_map.73 = f32[8,2048]{1,0:T(8,128)S(1)} custom-call(s32[1]{0:T(128)S(6)} %copy.10.length_ref, s32[8,16]{1,0:T(8,128)} %mask_hbm.1, f32[8,2048]{1,0:T(8,128)} %obs_hbm.1, f32[1,2048]{1,0:T(1,128)} %bitcast.1, f32[16,128,128]{2,1,0:T(8,128)} %trans_hbm.1, f32[16,128,128]{2,1,0:T(8,128)} %filt_hbm.1, f32[16,128,128]{2,1,0:T(8,128)} %smooth_hbm.1), custom_call_target="tpu_custom_call" | custom-call | tf_op jit(solution)/shard_map/pallas_call | solution.py:459
  22.2 0.6 %copy.9 = f32[8,2048]{1,0:T(8,128)} copy(f32[8,2048]{1,0:T(8,128)S(1)} %shard_map.73) | data formatting | bytes 131072

commit v6 on v3

--- a/solution.py
+++ b/solution.py
@@ -157,7 +157,6 @@
     trans_t = trans.T
     update_t = update.T
     gain_t = ready(gain.T)
-    step_t = ready(jnp.concatenate([update_t, trans_t], axis=1))
     square = mm(
         jnp.concatenate([trans, update], axis=0),
         ready(jnp.concatenate([trans, update], axis=1)),
@@ -172,6 +171,7 @@
 
     pairs = [tile(square, hi, lo) for hi in range(2) for lo in range(2)]
     pairs_t = [tile(square_t, lo, hi) for hi in range(2) for lo in range(2)]
+    moves = ready(jnp.concatenate([update_t, trans_t] + pairs_t, axis=1))
     cube = mm(
         jnp.concatenate([trans, update], axis=0), ready(jnp.concatenate(pairs, axis=1))
     )
@@ -222,13 +222,23 @@
         for s in range(WORD)
     ]
 
-    def advance(state, s):
-        both = mm(state, step_t)
-        return jnp.where(seen[s], both[:, :width], both[:, width:]) + gains[s]
-
-    offset = gains[0]
-    for s in range(1, WORD):
-        offset = advance(offset, s)
+    def part(rows, place):
+        return rows[:, place * width : (place + 1) * width]
+
+    def one_step(moved, now):
+        return jnp.where(now, part(moved, 0), part(moved, 1))
+
+    def two_steps(moved, now, later):
+        return jnp.where(
+            later,
+            jnp.where(now, part(moved, 5), part(moved, 4)),
+            jnp.where(now, part(moved, 3), part(moved, 2)),
+        )
+
+    moved = mm(jnp.concatenate(gains[:2], axis=0), moves)
+    middle = one_step(moved[:chunks], seen[1]) + gains[1]
+    offset = two_steps(moved[:chunks], seen[1], seen[2]) + one_step(moved[chunks:], seen[2])
+    offset = offset + gains[2]
     offsets[...] = offset
     index_copy.wait()
 
@@ -274,12 +284,12 @@
     for _ in side:
         pass
 
-    state = entries[0:chunks, :]
-    filtered = []
-    for s in range(WORD - 1):
-        state = advance(state, s)
-        filtered.append(state)
-    filtered.append(entries[1 : chunks + 1, :])
+    moved = mm(entries[0:chunks, :], moves)
+    filtered = [
+        one_step(moved, seen[0]) + gains[0],
+        two_steps(moved, seen[0], seen[1]) + middle,
+        entries[1 : chunks + 1, :],
+    ]
     newest = entries[chunks : chunks + 1, :]
 
     tail = buf_a.shape[1] - chunks

time: 21 us -> 20.9 us (level)
  no operation moved by 1% of the time
where the time goes in v6:
time: 20.9 us; the launch traced here: 20.7 us
  Pallas kernels  19.4 us (93%)
  between operations  0.66 us (3%)
  local copies, waits for them, and re-layouts  0.63 us (3%)
    pallas_call x1, Pallas kernels, shards(): pl.pallas_call(functools.partial(kernel, n), out_shape=pltpu.VMEM(observa...  19.4 us
    unnamed x1, local copies, waits for them, and re-layouts  0.63 us

profile of v6, /device:TPU:0, one launch (start us, length us, event | category | flops | bytes accessed | tf_op | source)
XLA Modules:
  0.0 20.7 jit_solution(8746863255572800341)
XLA Ops:
  0.7 19.4 %shard_map.73 = f32[8,2048]{1,0:T(8,128)S(1)} custom-call(s32[1]{0:T(128)S(6)} %copy.10.length_ref, s32[8,16]{1,0:T(8,128)} %mask_hbm.1, f32[8,2048]{1,0:T(8,128)} %obs_hbm.1, f32[1,2048]{1,0:T(1,128)} %bitcast.1, f32[16,128,128]{2,1,0:T(8,128)} %trans_hbm.1, f32[16,128,128]{2,1,0:T(8,128)} %filt_hbm.1, f32[16,128,128]{2,1,0:T(8,128)} %smooth_hbm.1), custom_call_target="tpu_custom_call" | custom-call | tf_op jit(solution)/shard_map/pallas_call | solution.py:366
  20.1 0.6 %copy.9 = f32[8,2048]{1,0:T(8,128)} copy(f32[8,2048]{1,0:T(8,128)S(1)} %shard_map.73) | data formatting | bytes 131072

commit v7 on v4

--- a/solution.py
+++ b/solution.py
@@ -9,7 +9,7 @@
 
 MESH = pl.DeviceIdType.MESH
 WORD = 3
-PER = 2
+PER = 1
 
 
 def split(value):

time: 21.6 us -> 22.6 us (1.046)
  Pallas kernels: 20.1 us -> 21.1 us
    pallas_call x1, Pallas kernels: 20.1 us -> 21.1 us  [shards(): pl.pallas_call(functools.partial(kernel, n), out_shape=pltpu.VMEM(observa...]
where the time goes in v7:
time: 22.6 us; the launch traced here: 22.4 us
  Pallas kernels  21.1 us (93%)
  between operations  0.66 us (3%)
  local copies, waits for them, and re-layouts  0.63 us (3%)
    pallas_call x1, Pallas kernels, shards(): pl.pallas_call(functools.partial(kernel, n), out_shape=pltpu.VMEM(observa...  21.1 us
    unnamed x1, local copies, waits for them, and re-layouts  0.63 us

profile of v7, /device:TPU:0, one launch (start us, length us, event | category | flops | bytes accessed | tf_op | source)
XLA Modules:
  0.0 22.4 jit_solution(3940271869330491156)
XLA Ops:
  0.7 21.1 %shard_map.73 = f32[8,2048]{1,0:T(8,128)S(1)} custom-call(s32[1]{0:T(128)S(6)} %copy.10.length_ref, s32[8,16]{1,0:T(8,128)} %mask_hbm.1, f32[8,2048]{1,0:T(8,128)} %obs_hbm.1, f32[1,2048]{1,0:T(1,128)} %bitcast.1, f32[16,128,128]{2,1,0:T(8,128)} %trans_hbm.1, f32[16,128,128]{2,1,0:T(8,128)} %filt_hbm.1, f32[16,128,128]{2,1,0:T(8,128)} %smooth_hbm.1), custom_call_target="tpu_custom_call" | custom-call | tf_op jit(solution)/shard_map/pallas_call | solution.py:417
  21.8 0.6 %copy.9 = f32[8,2048]{1,0:T(8,128)} copy(f32[8,2048]{1,0:T(8,128)S(1)} %shard_map.73) | data formatting | bytes 131072
